TPU v7x, 512 devices: a whole 4x4x16 slice. The times are simulated.
512 devices in a mesh: client: 32 (over x, y, core), dp: 16 (over z).
Axes of the slice: x: 4, y: 4, z: 16, core: 2. Of those that a mesh axis runs over, the one named last changes fastest.
Arguments:
- hidden: bfloat16 [32, 2048, 14336], P('client', 'dp'), may hold values from -6 to 6
- frozen_residual: bfloat16 [32, 2048, 64], P('client', 'dp'), may hold values from -6 to 6
- head: bfloat16 [32, 64, 4096], P('client'), may hold values from -0.09375 to 0.09375
- global_input_factor: bfloat16 [16, 14336], replicated, may hold values from -0.046875 to 0.046875
- global_output_factor: bfloat16 [16, 4096], replicated, may hold values from -0.119628906 to 0.119628906
- counts: int32 [32, 16], P('client', 'dp'), may hold values from 32 to 128, as said below
- weights: int32 [32], P('client'), may hold values from 1 to 8
- input_privacy_noise: float32 [16, 14336], P(None, 'dp'), may hold values from -6 to 6
- output_privacy_noise: float32 [16, 4096], P(None, 'dp'), may hold values from -6 to 6
Outputs:
- update_in: float32 [16, 14336], P(None, 'dp')
- update_out: float32 [16, 4096], P(None, 'dp')
Inputs may be any that keep to these rules, and one draw needn't show every extreme that they name: `counts`: the live tokens of a device are its first rows; in every client some device has all 128 slots live.
All inputs are finite; a program needn't handle non-finite values.
Results may differ from a plain program's by a relative error of at most 0.0011.
Values sent between devices are 32-bit elements; how exact they have to be, the bound alone decides.
A program may use at most 64 MiB of HBM per device.

v0:
```python
import math

import jax
import jax.numpy as jnp
from jax import lax
from jax.sharding import PartitionSpec as P

MODEL_WIDTH = 4096
HIDDEN_UNITS = 14336
ADAPTER_RANK = 16
ITERS = 3


learn_rate = 0.1
clip_bound = 0.001
noise_mult = 0.1


def local_grads(client_rows, resid_zero, head_wide, mask, total, adapt_in, adapt_out):
    high = lax.Precision.HIGHEST
    proj = lax.dot_general(
        client_rows,
        adapt_in.astype(jnp.bfloat16),
        (((1,), (1,)), ((), ())),
        preferred_element_type=jnp.float32,
    )
    mixed = jnp.dot(adapt_out, head_wide.T, precision=high)
    resid = resid_zero + jnp.dot(proj, mixed, precision=high)
    dres = resid * mask / total
    dproj = jnp.dot(dres, mixed.T, precision=high).astype(jnp.bfloat16)
    grad_in = lax.dot_general(
        dproj, client_rows, (((0,), (0,)), ((), ())), preferred_element_type=jnp.float32
    )
    inner = jnp.dot(proj.T, dres, precision=high)
    return (grad_in, inner)


def on_device(
    hidden,
    frozen_residual,
    head,
    global_input_factor,
    global_output_factor,
    counts,
    weights,
    input_privacy_noise,
    output_privacy_noise,
):
    high = lax.Precision.HIGHEST
    client_rows = hidden[0]
    resid_zero = frozen_residual[0].astype(jnp.float32)
    head_wide = head[0].astype(jnp.float32)
    active_rows = counts[0, 0]
    slots = client_rows.shape[0]
    mask = (lax.iota(jnp.int32, slots) < active_rows).astype(jnp.float32)[:, None]
    total = lax.psum(active_rows.astype(jnp.float32), "dp")
    initial_input_factor = global_input_factor.astype(jnp.float32)
    initial_output_factor = global_output_factor.astype(jnp.float32)
    adapt_in, adapt_out = (initial_input_factor, initial_output_factor)
    width_in = input_privacy_noise.shape[1]
    width_out = output_privacy_noise.shape[1]
    position = lax.axis_index("dp")
    for step in range(ITERS):
        grad_in, inner = local_grads(
            client_rows, resid_zero, head_wide, mask, total, adapt_in, adapt_out
        )
        grad_out = jnp.dot(inner, head_wide, precision=high)
        summed_in, summed_out = lax.psum((grad_in, grad_out), "dp")
        adapt_in = adapt_in - learn_rate * summed_in
        adapt_out = adapt_out - learn_rate * summed_out
    input_factor_change = adapt_in - initial_input_factor
    output_factor_change = adapt_out - initial_output_factor
    local_in = lax.dynamic_slice_in_dim(input_factor_change, position * width_in, width_in, 1)
    local_out = lax.dynamic_slice_in_dim(output_factor_change, position * width_out, width_out, 1)
    squares = lax.psum(jnp.sum(local_in * local_in) + jnp.sum(local_out * local_out), "dp")
    factor_matrix = jnp.minimum(1.0, clip_bound / jnp.sqrt(squares + 1e-06))
    weight = weights[0].astype(jnp.float32)
    scale = weight * factor_matrix
    agg_in, agg_out, wsum = lax.psum((scale * local_in, scale * local_out, weight), "client")
    out_scale = math.sqrt(ADAPTER_RANK * (HIDDEN_UNITS + MODEL_WIDTH)) / clip_bound
    update_in = (agg_in + noise_mult * clip_bound * input_privacy_noise) * out_scale / wsum
    update_out = (agg_out + noise_mult * clip_bound * output_privacy_noise) * out_scale / wsum
    return (update_in, update_out)


def solution(mesh):
    in_specs = (
        P("client", "dp", None),
        P("client", "dp", None),
        P("client", None, None),
        P(),
        P(),
        P("client", "dp"),
        P("client"),
        P(None, "dp"),
        P(None, "dp"),
    )
    out_specs = (P(None, "dp"), P(None, "dp"))
    return jax.shard_map(
        on_device, mesh=mesh, in_specs=in_specs, out_specs=out_specs, check_vma=False
    )
```

profile of v0, /device:TPU:1, one launch (start us, length us, event | category | flops | bytes accessed | tf_op | source)
XLA Modules:
  0.0 643.3 jit_solution(4498655267884734511)
XLA Ops:
  7.2 0.0 copy-start
  7.2 0.0 all-reduce.13.cloned.1.call-start
  7.9 30.9 %psum.77 = f32[]{:T(128)} all-reduce(f32[]{:T(128)S(6)} %convert_element_type.51), channel_id=1, replica_groups=mesh['client'=32,'dp'=16] {'dp'}, use_global_device_ids=true, to_apply=%region_0.0 | all-reduce | flops 1 | bytes 8 | tf_op jit(solution)/shard_map/psum | solution.py:56
  38.8 3.3 fusion.10
  42.1 0.0 copy-done
  42.1 0.0 copy-done.6
  42.1 0.2 fusion.28
  42.4 0.9 fusion.17
  43.3 0.3 convolution_convert_fusion.2
  43.6 0.1 fusion.36
  43.7 0.0 copy-done.1
  43.7 0.0 copy-start.4
  43.8 1.6 fusion.8
  45.4 1.0 fusion.26
  46.4 0.0 all-reduce.13.cloned.1.call-update
  46.4 0.0 all-reduce.11.cloned.1.call-start
  46.5 133.5 %all-reduce.13.cloned.1.call-done = (f32[16,14336]{1,0:T(8,128)}, f32[16,4096]{1,0:T(8,128)}) async-done(((f32[16,14336]{1,0:T(8,128)}, f32[16,4096]{1,0:T(8,128)}), (f32[16,14336]{1,0:T(8,128)}, f32[16,4096]{1,0:T(8,128)})) %all-reduce.13.cloned.1.call-update) | async-done | bytes 1179664 | tf_op jit(solution)/shard_map/psum | solution.py:68
  180.0 1.6 fusion.24
  181.6 0.0 copy-done.4
  181.6 3.4 fusion.6
  185.0 0.9 fusion.15
  185.9 0.1 fusion.37
  186.0 0.3 convolution_convert_fusion.1
  186.4 1.0 fusion.22
  187.4 1.6 fusion.4
  189.0 0.0 all-reduce.11.cloned.1.call-update
  189.0 0.0 all-reduce.9.cloned.1.call-start
  189.1 136.4 %all-reduce.11.cloned.1.call-done = (f32[16,14336]{1,0:T(8,128)}, f32[16,4096]{1,0:T(8,128)}) async-done(((f32[16,14336]{1,0:T(8,128)}, f32[16,4096]{1,0:T(8,128)}), (f32[16,14336]{1,0:T(8,128)}, f32[16,4096]{1,0:T(8,128)})) %all-reduce.11.cloned.1.call-update) | async-done | bytes 1179664 | tf_op jit(solution)/shard_map/psum | solution.py:68
  325.5 1.2 multiply_subtract_fusion.3
  326.6 0.5 fusion.20
  327.1 0.0 copy-done.5
  327.2 1.4 multiply_subtract_fusion
  328.5 1.0 fusion.2
  329.6 0.9 fusion.13
  330.5 0.1 fusion.38
  330.6 0.3 convolution_convert_fusion
  331.0 1.0 fusion.18
  332.0 1.6 fusion
  333.6 0.0 all-reduce.9.cloned.1.call-update
  333.7 0.1 convert_element_type.47
  334.4 135.8 %all-reduce.9.cloned.1.call-done = (f32[16,14336]{1,0:T(8,128)}, f32[16,4096]{1,0:T(8,128)}) async-done(((f32[16,14336]{1,0:T(8,128)}, f32[16,4096]{1,0:T(8,128)}), (f32[16,14336]{1,0:T(8,128)}, f32[16,4096]{1,0:T(8,128)})) %all-reduce.9.cloned.1.call-update) | async-done | bytes 1179664 | tf_op jit(solution)/shard_map/psum | solution.py:68
  470.2 1.3 multiply_reduce_fusion.1
  471.5 1.4 multiply_reduce_fusion
  474.2 22.1 %psum.84 = f32[]{:T(128)} all-reduce(f32[]{:T(128)S(6)} %add.54), channel_id=1, replica_groups=mesh['client'=32,'dp'=16] {'dp'}, use_global_device_ids=true, to_apply=%region_9.0 | all-reduce | flops 1 | bytes 8 | tf_op jit(solution)/shard_map/psum | solution.py:75
  497.0 137.4 %all-reduce.14 = (f32[16,896]{1,0:T(8,128)S(1)}, f32[]{:T(128)}, f32[16,256]{1,0:T(8,128)S(1)}) all-reduce(f32[16,896]{1,0:T(8,128)S(1)} %broadcast_multiply_fusion, f32[]{:T(128)} %bitcast, f32[16,256]{1,0:T(8,128)S(1)} %broadcast_multiply_fusion.1), channel_id=1, replica_groups=mesh['client'=32,'dp'=16] {'client'}, use_global_device_ids=true, to_apply=%region_10.0 | all-reduce | flops 18433 | bytes 147464 | tf_op jit(solution)/shard_map/psum | solution.py:79
  634.4 0.0 copy-done.9
  634.4 1.2 multiply_divide_fusion.1
  635.6 1.2 multiply_divide_fusion
  (18 shorter events, 0.1 us)
Async XLA Ops:
  7.2 35.0 %copy-start = (bf16[1,64,4096]{2,1,0:T(8,128)(2,1)S(1)}, bf16[1,64,4096]{2,1,0:T(8,128)(2,1)}, u32[]{:S(2)}) copy-start(bf16[1,64,4096]{2,1,0:T(8,128)(2,1)} %param.11) | copy-start | bytes 1572868
  7.2 35.0 %copy-start.6 = (bf16[16,4096]{1,0:T(8,128)(2,1)S(1)}, bf16[16,4096]{1,0:T(8,128)(2,1)}, u32[]{:S(2)}) copy-start(bf16[16,4096]{1,0:T(8,128)(2,1)} %param.13) | copy-start | bytes 393220
  7.2 35.2 %copy-start.10 = (bf16[1,128,64]{1,2,0:T(8,128)(2,1)S(1)}, bf16[1,128,64]{1,2,0:T(8,128)(2,1)}, u32[]{:S(2)}) copy-start(bf16[1,128,64]{1,2,0:T(8,128)(2,1)} %param.10) | copy-start | bytes 49156
  7.2 172.8 %all-reduce.13.cloned.1.call-start = ((), (), s32[]{:S(2)}) async-start(), calls=%async_computation.2 | async-start | bytes 2359296 | tf_op jit(solution)/shard_map/psum | solution.py:68
  38.8 4.9 copy-start.1
  43.7 137.8 %copy-start.4 = (bf16[16,14336]{1,0:T(8,128)(2,1)S(1)}, bf16[16,14336]{1,0:T(8,128)(2,1)}, u32[]{:S(2)}) copy-start(bf16[16,14336]{1,0:T(8,128)(2,1)} %param.12) | copy-start | bytes 1376260
  46.4 279.1 %all-reduce.11.cloned.1.call-start = ((), (), s32[]{:S(2)}) async-start(), calls=%async_computation.1 | async-start | bytes 2359296 | tf_op jit(solution)/shard_map/psum | solution.py:68
  180.0 7.5 %copy-start.2 = (bf16[1,128,14336]{2,1,0:T(8,128)(2,1)S(1)}, bf16[1,128,14336]{2,1,0:T(8,128)(2,1)}, u32[]{:S(2)}) copy-start(bf16[1,128,14336]{2,1,0:T(8,128)(2,1)} %param.9) | copy-start | bytes 11010052
  185.0 140.5 %copy-start.7 = (f32[16,4096]{1,0:T(8,128)S(1)}, f32[16,4096]{1,0:T(8,128)}, u32[]{:S(2)}) copy-start(f32[16,4096]{1,0:T(8,128)} %get-tuple-element.10) | copy-start | bytes 786436
  187.4 139.7 %copy-start.5 = (f32[16,14336]{1,0:T(8,128)S(1)}, f32[16,14336]{1,0:T(8,128)}, u32[]{:S(2)}) copy-start(f32[16,14336]{1,0:T(8,128)} %get-tuple-element.9) | copy-start | bytes 2752516
  189.0 281.2 %all-reduce.9.cloned.1.call-start = ((), (), s32[]{:S(2)}) async-start(), calls=%async_computation | async-start | bytes 2359296 | tf_op jit(solution)/shard_map/psum | solution.py:68
  325.5 3.1 copy-start.3
  332.0 302.4 %copy-start.9 = (f32[16,256]{1,0:T(8,128)S(1)}, f32[16,256]{1,0:T(8,128)}, u32[]{:S(2)}) copy-start(f32[16,256]{1,0:T(8,128)} %param.17) | copy-start | bytes 49156
  332.0 303.6 %copy-start.8 = (f32[16,896]{1,0:T(8,128)S(1)}, f32[16,896]{1,0:T(8,128)}, u32[]{:S(2)}) copy-start(f32[16,896]{1,0:T(8,128)} %param.16) | copy-start | bytes 172036
Sparse Core Ops, SparseCore 0:
  46.5 133.3 all-reduce.12
  189.1 136.2 all-reduce.10
  333.7 136.3 all-reduce.8
where the time goes:
time: 645 us; the launch traced here: 643 us
  waiting for transfers between devices  406 us (63%)
  blocking collectives  190 us (29%)
  matrix products  22 us (3%)
  between operations  17.3 us (3%)
  other arithmetic  7.77 us (1%)
    psum x3, waiting for transfers between devices, on_device(): summed_in, summed_out = lax.psum((grad_in, grad_out), 'dp')  406 us
    psum x1, blocking collectives, on_device(): lax.psum((scale * local_in, scale * local_out, weight), 'client')  137 us
    psum x1, blocking collectives, on_device(): total = lax.psum(active_rows.astype(jnp.float32), 'dp')  30.9 us
    psum x1, blocking collectives, on_device(): lax.psum(jnp.sum(local_in * local_in) + jnp.sum(local_out * local_out), '...  22.1 us
  transfers between devices with their start and end apart: 3, of which 3 were waited for; matrix products, arithmetic and copies ran while one was open for 0% of the time, Pallas kernels for 0%

commit v1 on v0

v1 whole, which is shorter than its diff:
```python
import functools
import math

import jax
import jax.numpy as jnp
from jax import lax
from jax.experimental import pallas as pl
from jax.experimental.pallas import tpu as pltpu
from jax.sharding import PartitionSpec as P

ITERS = 3
CORES = 2

learn_rate = 0.1
clip_bound = 0.001
noise_mult = 0.1

MESH = pl.DeviceIdType.MESH
HIGH = lax.Precision.HIGHEST
NN = (((1,), (0,)), ((), ()))
NT = (((1,), (1,)), ((), ()))
TN = (((0,), (0,)), ((), ()))


def mm(a, b, dims=NN, precision=None):
    return lax.dot_general(
        a, b, dims, precision=precision, preferred_element_type=jnp.float32
    )


def kernel(
    n,
    clients,
    out_scale,
    hid_ref,
    res_ref,
    head_ref,
    a0_ref,
    b0_ref,
    cnt_ref,
    w_ref,
    nin_ref,
    nout_ref,
    oin_ref,
    oout_ref,
    hv,
    grad,
    slot,
    a_all,
    own,
    part,
    spread,
    row_out,
    row_in,
    pair,
    row_done,
    hid_sem,
    rs_send,
    rs_recv,
    ag_send,
    ag_recv,
    pt_send,
    pt_recv,
    sc_send,
    sc_recv,
    ro_send,
    ro_recv,
    pr_send,
    pr_recv,
    rd_send,
    rd_recv,
):
    half_n = n // 2
    chips = clients // CORES
    rank, width_in = nin_ref.shape
    width_out = nout_ref.shape[1]
    half = rank // 2
    nout = head_ref.shape[0]
    tokens = hv.shape[1]
    width = width_in + width_out

    z = lax.axis_index("dp")
    client = lax.axis_index("client")
    chip = lax.div(client, CORES)
    core = lax.rem(client, CORES)
    twin = chip * CORES + (1 - core)
    ring = (lax.rem(z + n - 1, n), lax.rem(z + 1, n))

    def at_z(k):
        return lax.rem(z + k, n)

    def at_chip(k):
        return lax.rem(chip + k, chips)

    barrier = pltpu.get_barrier_semaphore()
    for k in range(1, n):
        pl.semaphore_signal(barrier, inc=1, device_id={"dp": at_z(k)}, device_id_type=MESH)
    for k in range(1, chips):
        pl.semaphore_signal(
            barrier, inc=1, device_id={"client": at_chip(k) * CORES + core}, device_id_type=MESH
        )
    pl.semaphore_signal(barrier, inc=1, device_id={"client": twin}, device_id_type=MESH)

    def load(j):
        return pltpu.make_async_copy(
            hid_ref.at[0, :, pl.ds(j * width_in, width_in)], hv.at[j], hid_sem.at[j]
        )

    for j in range(n):
        load(j).start()

    head = head_ref[...]
    gram = mm(head, head, NT)
    mixed = mm(b0_ref[...], head, NT)
    mixed_t = mm(head, b0_ref[...], NT)
    base_t = res_ref[...].astype(jnp.float32).T
    lane = lax.broadcasted_iota(jnp.int32, (1, tokens), 1)
    live = cnt_ref[0, 0]
    mask = (lane < live).astype(jnp.float32)

    pl.semaphore_wait(barrier, (n - 1) + (chips - 1) + 1)

    def z_copy(which, k):
        return pltpu.make_async_remote_copy(
            src_ref=spread.at[which, z],
            dst_ref=spread.at[which, z],
            send_sem=sc_send.at[which, k],
            recv_sem=sc_recv.at[which, k],
            device_id={"dp": at_z(k)},
            device_id_type=MESH,
        )

    def z_start(which, row):
        spread[which, z] = row
        for k in range(1, n):
            z_copy(which, k).start()

    def z_finish(which):
        for k in range(1, n):
            z_copy(which, k).wait()
        total = spread[which, 0]
        for j in range(1, n):
            total = total + spread[which, j]
        return total

    z_start(0, jnp.full((1, 128), live.astype(jnp.float32), jnp.float32))

    proj = jnp.zeros((rank, tokens), jnp.float32)
    for j in range(n):
        load(j).wait()
        proj = proj + mm(a0_ref[:, j * width_in : (j + 1) * width_in], hv[j], NT)

    tokens_live = z_finish(0)[:, :1]

    start_cols = pl.ds(pl.multiple_of(z * width_in, 128), width_in)
    own_zero = a0_ref[:, start_cols].astype(jnp.float32)
    for h in range(2):
        own[h] = own_zero[h * half : (h + 1) * half]

    def rs_copy(it, way, h, s, owner):
        return pltpu.make_async_remote_copy(
            src_ref=grad.at[it, owner, h],
            dst_ref=slot.at[it, way, h, s],
            send_sem=rs_send.at[it, way, h, s],
            recv_sem=rs_recv.at[it, way, h, s],
            device_id={"dp": ring[way]},
            device_id_type=MESH,
        )

    def ag_copy(it, way, h, t, owner):
        return pltpu.make_async_remote_copy(
            src_ref=a_all.at[it, owner, h],
            dst_ref=a_all.at[it, owner, h],
            send_sem=ag_send.at[it, way, h, t],
            recv_sem=ag_recv.at[it, way, h, t],
            device_id={"dp": ring[way]},
            device_id_type=MESH,
        )

    def pt_copy(it, way, t, owner):
        return pltpu.make_async_remote_copy(
            src_ref=part.at[it, owner],
            dst_ref=part.at[it, owner],
            send_sem=pt_send.at[it, way, t],
            recv_sem=pt_recv.at[it, way, t],
            device_id={"dp": ring[way]},
            device_id_type=MESH,
        )

    def long(way, h):
        return way == h

    inner_sum = jnp.zeros((rank, nout), jnp.float32)
    for it in range(ITERS):
        last = it == ITERS - 1
        resid = base_t + mm(mixed_t, proj, NN, HIGH)
        dres = resid * mask / tokens_live
        dproj = mm(mixed, dres, NN, HIGH).astype(jnp.bfloat16)

        def local(owner):
            value = mm(dproj, hv[owner])
            for h in range(2):
                grad[it, owner, h] = value[h * half : (h + 1) * half]

        far = at_z(half_n)
        local(far)
        for way in range(2):
            rs_copy(it, way, way, 0, far).start()

        inner = mm(proj, dres, NT, HIGH)
        part[it, z] = jnp.concatenate([inner[:half], inner[half:]], axis=1)
        for way in range(2):
            pt_copy(it, way, 0, z).start()

        for s in range(1, half_n):
            k = half_n - s
            owners = (at_z(n - k), at_z(k))
            for way in range(2):
                local(owners[way])
            for h in range(2):
                for way in range(2):
                    if s > 1 or long(way, h):
                        rs_copy(it, way, h, s - 1, owners[way]).wait_recv()
                        grad[it, owners[way], h] += slot[it, way, h, s - 1]
                    rs_copy(it, way, h, s, owners[way]).start()
            for way in range(2):
                source = at_z(s) if way == 0 else at_z(n - s)
                pt_copy(it, way, s - 1, source).wait_recv()
                if s < half_n - 1 or way == 0:
                    pt_copy(it, way, s, source).start()
        local(z)
        for h in range(2):
            for way in range(2):
                rs_copy(it, way, h, half_n - 1, z).wait_recv()
            total = grad[it, z, h] + (slot[it, 0, h, half_n - 1] + slot[it, 1, h, half_n - 1])
            own[h] = own[h] - learn_rate * total
            if not last:
                a_all[it, z, h] = own[h]
                for way in range(2):
                    ag_copy(it, way, h, 0, z).start()
        pt_copy(it, 0, half_n - 1, far).wait_recv()
        tile = part[it, 0]
        for j in range(1, n):
            tile = tile + part[it, j]
        step_inner = jnp.concatenate([tile[:, :nout], tile[:, nout:]], axis=0)
        inner_sum = inner_sum + step_inner

        if not last:
            mixed = mixed - learn_rate * mm(step_inner, gram, NN, HIGH)
            mixed_t = mixed_t - learn_rate * mm(gram, step_inner, NT, HIGH)

            def project(owner):
                rows = jnp.concatenate([a_all[it, owner, 0], a_all[it, owner, 1]], axis=0)
                return mm(rows.astype(jnp.bfloat16), hv[owner], NT)

            proj = project(z)
            for t in range(1, half_n):
                sources = (at_z(t), at_z(n - t))
                for h in range(2):
                    for way in range(2):
                        ag_copy(it, way, h, t - 1, sources[way]).wait_recv()
                        if t < half_n - 1 or long(way, h):
                            ag_copy(it, way, h, t, sources[way]).start()
                for way in range(2):
                    proj = proj + project(sources[way])
            for way in range(2):
                ag_copy(it, way, way, half_n - 1, far).wait_recv()
            proj = proj + project(far)

    own_three = jnp.concatenate([own[0], own[1]], axis=0)
    delta_in = own_three - own_zero
    out_cols = pl.ds(pl.multiple_of(z * width_out, 128), width_out)
    head_cols = head_ref[:, out_cols].astype(jnp.float32)
    delta_out = -learn_rate * mm(inner_sum, head_cols, NN, HIGH)
    delta = jnp.concatenate([delta_in, delta_out], axis=1)
    sums = jnp.sum(delta * delta, axis=0, keepdims=True)
    lanes = sums[:, :128]
    for j in range(1, width // 128):
        lanes = lanes + sums[:, j * 128 : (j + 1) * 128]
    z_start(1, lanes)
    squares = jnp.sum(z_finish(1), axis=1, keepdims=True)
    factor = jnp.minimum(1.0, clip_bound / jnp.sqrt(squares + 1e-06))
    weight = w_ref[0].astype(jnp.float32)
    scaled = delta * (factor * weight)

    weight_row = jnp.full((1, 128), weight, jnp.float32)
    for r in range(rank):
        row_out[r] = jnp.concatenate([scaled[r : r + 1], weight_row], axis=1)

    def ro_copy(k):
        return pltpu.make_async_remote_copy(
            src_ref=row_out.at[at_chip(k)],
            dst_ref=row_in.at[chip],
            send_sem=ro_send.at[k],
            recv_sem=ro_recv.at[k],
            device_id={"client": at_chip(k) * CORES + core},
            device_id_type=MESH,
        )

    for k in range(1, chips):
        ro_copy(k).start()
    row_in[chip] = row_out[chip]
    for k in range(1, chips):
        ro_copy(k).wait()
    row = row_in[0]
    for j in range(1, chips):
        row = row + row_in[j]
    pair[0] = row
    pr_copy = pltpu.make_async_remote_copy(
        src_ref=pair.at[0],
        dst_ref=pair.at[1],
        send_sem=pr_send,
        recv_sem=pr_recv,
        device_id={"client": twin},
        device_id_type=MESH,
    )
    pr_copy.start()
    noise = jnp.concatenate(
        [nin_ref[pl.ds(chip, 1), :], nout_ref[pl.ds(chip, 1), :]], axis=1
    )
    pr_copy.wait()
    row = pair[0] + pair[1]
    wsum = row[:, width : width + 1]
    row_done[chip] = (row[:, :width] + noise_mult * clip_bound * noise) * out_scale / wsum

    def rd_copy(k):
        return pltpu.make_async_remote_copy(
            src_ref=row_done.at[chip],
            dst_ref=row_done.at[chip],
            send_sem=rd_send.at[k],
            recv_sem=rd_recv.at[k],
            device_id={"client": at_chip(k) * CORES + core},
            device_id_type=MESH,
        )

    for k in range(1, chips):
        rd_copy(k).start()

    for it in range(ITERS):
        for s in range(half_n):
            for way in range(2):
                for h in range(2):
                    if s > 0 or long(way, h):
                        rs_copy(it, way, h, s, z).wait_send()
                    if it < ITERS - 1 and (s < half_n - 1 or long(way, h)):
                        ag_copy(it, way, h, s, z).wait_send()
                if s < half_n - 1 or way == 0:
                    pt_copy(it, way, s, z).wait_send()

    for k in range(1, chips):
        rd_copy(k).wait()
    for r in range(rank):
        row = row_done[r]
        oin_ref[r : r + 1, :] = row[:, :width_in]
        oout_ref[r : r + 1, :] = row[:, width_in:]


def on_device(
    n,
    clients,
    hidden,
    frozen_residual,
    head,
    global_input_factor,
    global_output_factor,
    counts,
    weights,
    input_privacy_noise,
    output_privacy_noise,
):
    tokens, hidden_units = hidden.shape[1:]
    rank, model_width = global_output_factor.shape
    width_in = input_privacy_noise.shape[1]
    width_out = output_privacy_noise.shape[1]
    half = rank // 2
    half_n = n // 2
    chips = clients // CORES
    width = width_in + width_out
    out_scale = math.sqrt(rank * (hidden_units + model_width)) / clip_bound
    f32 = jnp.float32
    dma = pltpu.SemaphoreType.DMA
    vmem = pl.BlockSpec(memory_space=pltpu.VMEM)
    smem = pl.BlockSpec(memory_space=pltpu.SMEM)
    return pl.pallas_call(
        functools.partial(kernel, n, clients, out_scale),
        out_shape=(
            jax.ShapeDtypeStruct((rank, width_in), f32),
            jax.ShapeDtypeStruct((rank, width_out), f32),
        ),
        in_specs=[
            pl.BlockSpec(memory_space=pl.ANY), vmem, vmem, vmem, vmem, smem, smem, vmem, vmem
        ],
        out_specs=(vmem, vmem),
        scratch_shapes=[
            pltpu.VMEM((n, tokens, width_in), jnp.bfloat16),
            pltpu.VMEM((ITERS, n, 2, half, width_in), f32),
            pltpu.VMEM((ITERS, 2, 2, half_n, half, width_in), f32),
            pltpu.VMEM((ITERS - 1, n, 2, half, width_in), f32),
            pltpu.VMEM((2, half, width_in), f32),
            pltpu.VMEM((ITERS, n, half, 128), f32),
            pltpu.VMEM((2, n, 1, 128), f32),
            pltpu.VMEM((rank, 1, width + 128), f32),
            pltpu.VMEM((chips, 1, width + 128), f32),
            pltpu.VMEM((2, 1, width + 128), f32),
            pltpu.VMEM((rank, 1, width), f32),
            dma((n,)),
            dma((ITERS, 2, 2, half_n)),
            dma((ITERS, 2, 2, half_n)),
            dma((ITERS - 1, 2, 2, half_n)),
            dma((ITERS - 1, 2, 2, half_n)),
            dma((ITERS, 2, half_n)),
            dma((ITERS, 2, half_n)),
            dma((2, n)),
            dma((2, n)),
            dma((chips,)),
            dma((chips,)),
            dma,
            dma,
            dma((chips,)),
            dma((chips,)),
        ],
        compiler_params=pltpu.CompilerParams(
            collective_id=0, has_side_effects=True, vmem_limit_bytes=48 * 1024 * 1024
        ),
    )(
        hidden,
        frozen_residual[0],
        head[0],
        global_input_factor,
        global_output_factor,
        counts,
        weights,
        input_privacy_noise,
        output_privacy_noise,
    )


def solution(mesh):
    in_specs = (
        P("client", "dp", None),
        P("client", "dp", None),
        P("client", None, None),
        P(),
        P(),
        P("client", "dp"),
        P("client"),
        P(None, "dp"),
        P(None, "dp"),
    )
    out_specs = (P(None, "dp"), P(None, "dp"))
    body = functools.partial(on_device, mesh.shape["dp"], mesh.shape["client"])
    return jax.shard_map(
        body, mesh=mesh, in_specs=in_specs, out_specs=out_specs, check_vma=False
    )
```

time: 645 us -> 191 us (0.30)
  waiting for transfers between devices: 406 us -> 0 us
  blocking collectives: 190 us -> 0 us
  Pallas kernels: 0 us -> 180 us
  matrix products: 22 us -> 0 us
  between operations: 17.3 us -> 1.95 us
  local copies, waits for them, and re-layouts: 0.08 us -> 8.59 us
  other arithmetic: 7.77 us -> 0 us
    psum x3 -> x0, waiting for transfers between devices: 406 us -> none  [on_device(): summed_in, summed_out = lax.psum((grad_in, grad_out), 'dp')]
    psum x3 -> x0, blocking collectives: 190 us -> none  [the longest x1 137 us: on_device(): lax.psum((scale * local_in, scale * local_out, weight), 'client')]
    pallas_call x0 -> x1, Pallas kernels: none -> 180 us  [on_device(): pl.pallas_call(functools.partial(kernel, n, clients, out_scale), out_shap...]
    dot_general x21 -> x0, matrix products: 22 us -> none  [the longest x3 7.74 us: local_grads(): lax.dot_general(client_rows, adapt_in.astype(jnp.bfloat16), (((1,), (1,))...]
    unnamed x22 -> x15, local copies, waits for them, and re-layouts: 0.08 us -> 8.59 us
  transfers between devices with their start and end apart: 3 -> 0, of which waited for: 3 -> 0; matrix products, arithmetic and copies ran while one was open for 0% -> 0% of each run, Pallas kernels for 0% -> 0%
where the time goes in v1:
time: 191 us; the launch traced here: 190 us
  Pallas kernels  180 us (94%)
  local copies, waits for them, and re-layouts  8.59 us (4%)
  between operations  1.95 us (1%)
    pallas_call x1, Pallas kernels, on_device(): pl.pallas_call(functools.partial(kernel, n, clients, out_scale), out_shap...  180 us
    unnamed x15, local copies, waits for them, and re-layouts  8.59 us

profile of v1, /device:TPU:1, one launch (start us, length us, event | category | flops | bytes accessed | tf_op | source)
XLA Modules:
  0.0 190.1 jit_solution(3996406307573628314)
XLA Ops:
  1.9 0.8 copy.11
  2.7 0.0 copy-start
  2.8 2.0 %copy-done = bf16[1,128,14336]{2,1,0:T(8,128)(2,1)S(1)} copy-done((bf16[1,128,14336]{2,1,0:T(8,128)(2,1)S(1)}, bf16[1,128,14336]{2,1,0:T(8,128)(2,1)}, u32[]{:S(2)}) %copy-start) | copy-done | bytes 3670040
  4.8 0.0 copy-start.1
  4.8 1.0 copy-done.1
  5.8 0.0 copy-start.2
  5.8 1.0 copy-done.2
  6.9 0.0 copy-start.3
  6.9 0.9 copy-done.3
  7.8 0.0 copy-start.4
  7.8 0.8 copy-done.4
  8.6 0.0 copy-start.5
  8.6 0.7 copy-done.5
  9.3 179.6 %shard_map.104 = (f32[16,896]{1,0:T(8,128)S(1)}, f32[16,256]{1,0:T(8,128)S(1)}) custom-call(bf16[1,128,14336]{2,1,0:T(8,128)(2,1)S(1)} %copy-done, bf16[128,64]{1,0:T(8,128)(2,1)S(1)} %bitcast.3, bf16[64,4096]{1,0:T(8,128)(2,1)S(1)} %bitcast.2, bf16[16,14336]{1,0:T(8,128)(2,1)S(1)} %copy-done.2, bf16[16,4096]{1,0:T(8,128)(2,1)S(1)} %copy-done.3, ...), custom_call_target="tpu_custom_call" | custom-call | tf_op jit(solution)/shard_map/pallas_call | solution.py:384
  188.9 0.6 copy.16
  189.5 0.6 copy.17
Async XLA Ops:
  2.7 2.0 %copy-start = (bf16[1,128,14336]{2,1,0:T(8,128)(2,1)S(1)}, bf16[1,128,14336]{2,1,0:T(8,128)(2,1)}, u32[]{:S(2)}) copy-start(bf16[1,128,14336]{2,1,0:T(8,128)(2,1)} %hid_ref.1) | copy-start | bytes 11010052
  4.8 1.0 copy-start.1
  5.8 1.0 copy-start.2
  6.9 0.9 copy-start.3
  7.8 0.8 copy-start.4
  8.6 0.7 copy-start.5

commit v2 on v1

v2 whole, which is shorter than its diff:
```python
import functools
import math

import jax
import jax.numpy as jnp
from jax import lax
from jax.experimental import pallas as pl
from jax.experimental.pallas import tpu as pltpu
from jax.sharding import PartitionSpec as P

ITERS = 3
CORES = 2

learn_rate = 0.1
clip_bound = 0.001
noise_mult = 0.1

MESH = pl.DeviceIdType.MESH
HIGH = lax.Precision.HIGHEST
NN = (((1,), (0,)), ((), ()))
NT = (((1,), (1,)), ((), ()))
TN = (((0,), (0,)), ((), ()))


def mm(a, b, dims=NN, precision=None):
    return lax.dot_general(
        a, b, dims, precision=precision, preferred_element_type=jnp.float32
    )


def kernel(
    n,
    clients,
    out_scale,
    hid_ref,
    res_hbm,
    head_hbm,
    a0_hbm,
    b0_hbm,
    cnt_ref,
    w_ref,
    nin_hbm,
    nout_hbm,
    oin_ref,
    oout_ref,
    res_ref,
    head_ref,
    a0_ref,
    b0_ref,
    nin_ref,
    nout_ref,
    hv,
    gram,
    mixed,
    mixed_t,
    inner_sum,
    mask,
    tokens_live,
    proj,
    dproj,
    square,
    base_in,
    grad,
    slot,
    a_all,
    own,
    part,
    spread,
    row_out,
    row_in,
    row_done,
    op_sem,
    hid_sem,
    rs_send,
    rs_recv,
    ag_send,
    ag_recv,
    pt_send,
    pt_recv,
    sc_send,
    sc_recv,
    ro_send,
    ro_recv,
    rd_send,
    rd_recv,
):
    half_n = n // 2
    stops = half_n // 2
    chips = clients // CORES
    rank, width_in = nin_ref.shape
    width_out = nout_ref.shape[1]
    half = rank // 2
    nout = head_ref.shape[0]
    tokens = hv.shape[1]
    width = width_in + width_out

    z = lax.axis_index("dp")
    client = lax.axis_index("client")
    chip = lax.div(client, CORES)
    core = lax.rem(client, CORES)
    ring = (
        (lax.rem(z + n - 2, n), lax.rem(z + 2, n)),
        (lax.rem(z + n - 1, n), lax.rem(z + 1, n)),
    )

    def at_z(k):
        return lax.rem(z + k, n)

    def at_chip(k):
        return lax.rem(chip + k, chips)

    def load(j):
        return pltpu.make_async_copy(
            hid_ref.at[0, :, pl.ds(j * width_in, width_in)], hv.at[j], hid_sem.at[j]
        )

    pieces = [
        pltpu.make_async_copy(src, dst, op_sem.at[i])
        for i, (src, dst) in enumerate(
            [
                (head_hbm, head_ref),
                (b0_hbm, b0_ref),
                (res_hbm, res_ref),
                (a0_hbm, a0_ref),
                (nin_hbm, nin_ref),
                (nout_hbm, nout_ref),
            ]
        )
    ]
    for piece in pieces[:4]:
        piece.start()
    for j in range(n):
        load(j).start()
    for piece in pieces[4:]:
        piece.start()

    barrier = pltpu.get_barrier_semaphore()
    for k in range(1, n):
        pl.semaphore_signal(barrier, inc=1, device_id={"dp": at_z(k)}, device_id_type=MESH)
    for k in range(1, clients):
        pl.semaphore_signal(
            barrier, inc=1, device_id={"client": lax.rem(client + k, clients)}, device_id_type=MESH
        )

    for piece in pieces[:3]:
        piece.wait()
    head = head_ref[...]
    gram[...] = mm(head, head, NT)
    mixed[...] = mm(b0_ref[...], head, NT)
    mixed_t[...] = mm(head, b0_ref[...], NT)
    inner_sum[...] = jnp.zeros_like(inner_sum)

    def from_mixed():
        square[...] = mm(mixed[...], mixed[...], NT, HIGH)
        base_in[...] = mm(mixed[...], res_ref[...].astype(jnp.float32), NN, HIGH)

    from_mixed()
    lane = lax.broadcasted_iota(jnp.int32, (1, tokens), 1)
    live = cnt_ref[0, 0]

    pl.semaphore_wait(barrier, (n - 1) + (clients - 1))

    def z_copy(which, k):
        return pltpu.make_async_remote_copy(
            src_ref=spread.at[which, z],
            dst_ref=spread.at[which, z],
            send_sem=sc_send.at[which, k],
            recv_sem=sc_recv.at[which, k],
            device_id={"dp": at_z(k)},
            device_id_type=MESH,
        )

    def z_start(which, row):
        spread[which, z] = row
        for k in range(1, n):
            z_copy(which, k).start()

    def z_finish(which):
        for k in range(1, n):
            z_copy(which, k).wait()
        total = spread[which, 0]
        for j in range(1, n):
            total = total + spread[which, j]
        return total

    z_start(0, jnp.full((1, 128), live.astype(jnp.float32), jnp.float32))

    pieces[3].wait()
    proj[...] = jnp.zeros_like(proj)

    def first(j, _):
        load(j).wait()
        cols = pl.ds(pl.multiple_of(j * width_in, 128), width_in)
        proj[...] += mm(hv[j], a0_ref[:, cols], NT)
        return 0

    lax.fori_loop(0, n, first, 0)

    start_cols = pl.ds(pl.multiple_of(z * width_in, 128), width_in)
    own_zero = a0_ref[:, start_cols].astype(jnp.float32)
    for h in range(2):
        own[h] = own_zero[h * half : (h + 1) * half]
    mask[...] = (lane < live).astype(jnp.float32)
    tokens_live[...] = z_finish(0)

    def rs_copy(it, way, h, odd, e, owner):
        return pltpu.make_async_remote_copy(
            src_ref=grad.at[it, owner, h],
            dst_ref=slot.at[it, way, h, odd, e],
            send_sem=rs_send.at[it, way, h, odd, e],
            recv_sem=rs_recv.at[it, way, h, odd, e],
            device_id={"dp": ring[odd][way]},
            device_id_type=MESH,
        )

    def ag_copy(it, way, h, odd, t, owner):
        return pltpu.make_async_remote_copy(
            src_ref=a_all.at[it, owner, h],
            dst_ref=a_all.at[it, owner, h],
            send_sem=ag_send.at[it, way, h, odd, t],
            recv_sem=ag_recv.at[it, way, h, odd, t],
            device_id={"dp": ring[odd][way]},
            device_id_type=MESH,
        )

    def pt_copy(it, way, odd, t, owner):
        return pltpu.make_async_remote_copy(
            src_ref=part.at[it, owner],
            dst_ref=part.at[it, owner],
            send_sem=pt_send.at[it, way, odd, t],
            recv_sem=pt_recv.at[it, way, odd, t],
            device_id={"dp": ring[odd][way]},
            device_id_type=MESH,
        )

    def long(way, h):
        return way == h

    far = at_z(half_n)

    def local_step(it, _):
        weighted = mask[...] / tokens_live[...]
        through = mm(square[...], proj[...], NT, HIGH)
        dproj[...] = ((base_in[...] + through) * weighted).astype(jnp.bfloat16)

        def local(owner):
            value = mm(dproj[...], hv[owner])
            for h in range(2):
                grad[it, owner, h] = value[h * half : (h + 1) * half]

        def beside(k):
            return at_z(n - k), at_z(k)

        def local_both(k):
            for owner in beside(k):
                local(owner)

        def send_odd(e):
            owners = beside(half_n - 1 - 2 * e)
            for h in range(2):
                for way in range(2):
                    rs_copy(it, way, h, 1, e, owners[way]).start()

        local(far)
        for way in range(2):
            rs_copy(it, way, way, 0, 0, far).start()
        local_both(half_n - 1)
        send_odd(0)
        local_both(half_n - 2)
        local_both(half_n - 3)
        send_odd(1)

        proj_t = proj[...].T
        resid = res_ref[...].astype(jnp.float32) + mm(mixed_t[...], proj_t, NN, HIGH)
        inner = mm(proj_t, resid * weighted, NT, HIGH)
        part[it, z] = jnp.concatenate([inner[:half], inner[half:]], axis=1)
        for odd in range(2):
            for way in range(2):
                pt_copy(it, way, odd, 0, z).start()

        for e in range(1, stops):
            owners = beside(half_n - 2 * e)
            for h in range(2):
                for way in range(2):
                    rs_copy(it, way, h, 1, e - 1, owners[way]).wait_recv()
                    total = grad[it, owners[way], h] + slot[it, way, h, 1, e - 1]
                    if long(way, h) or e > 1:
                        rs_copy(it, way, h, 0, e - 1, owners[way]).wait_recv()
                        total = total + slot[it, way, h, 0, e - 1]
                    grad[it, owners[way], h] = total
                    rs_copy(it, way, h, 0, e, owners[way]).start()
            if e < stops - 1:
                local_both(half_n - 2 * e - 2)
                local_both(half_n - 2 * e - 3)
                send_odd(e + 1)
            else:
                local(z)
            for way in range(2):
                source = at_z(2 * e) if way == 0 else at_z(n - 2 * e)
                pt_copy(it, way, 0, e - 1, source).wait_recv()
                if way == 0 or e < stops - 1:
                    pt_copy(it, way, 0, e, source).start()
                pt_copy(it, way, 1, e, source).start()
                pt_copy(it, way, 1, e - 1, source).wait_recv()
        for h in range(2):
            total = grad[it, z, h]
            for odd in (1, 0):
                for way in range(2):
                    rs_copy(it, way, h, odd, stops - 1, z).wait_recv()
                    total = total + slot[it, way, h, odd, stops - 1]
            own[h] = own[h] - learn_rate * total

            @pl.when(it < ITERS - 1)
            def _():
                a_all[it, z, h] = own[h]
                for way in range(2):
                    ag_copy(it, way, h, 0, 0, z).start()

        @pl.when(it < ITERS - 1)
        def _():
            for h in range(2):
                for way in range(2):
                    ag_copy(it, way, h, 1, 0, z).start()

        pt_copy(it, 0, 0, stops - 1, far).wait_recv()
        for way in range(2):
            pt_copy(it, way, 1, stops - 1, far).wait_recv()
        tile = part[it, 0]
        for j in range(1, n):
            tile = tile + part[it, j]
        step_inner = jnp.concatenate([tile[:, :nout], tile[:, nout:]], axis=0)
        inner_sum[...] += step_inner

        @pl.when(it < ITERS - 1)
        def _():
            mixed[...] = mixed[...] - learn_rate * mm(step_inner, gram[...], NN, HIGH)
            mixed_t[...] = mixed_t[...] - learn_rate * mm(gram[...], step_inner, NT, HIGH)
            from_mixed()

            def project(owner):
                rows = jnp.concatenate([a_all[it, owner, 0], a_all[it, owner, 1]], axis=0)
                return mm(hv[owner], rows.astype(jnp.bfloat16), NT)

            proj[...] = project(z)

            for t in range(1, stops):
                sources = (at_z(2 * t), at_z(n - 2 * t))
                between = (at_z(2 * t - 1), at_z(n - 2 * t + 1))
                for h in range(2):
                    for way in range(2):
                        ag_copy(it, way, h, 0, t - 1, sources[way]).wait_recv()
                        if long(way, h) or t < stops - 1:
                            ag_copy(it, way, h, 0, t, sources[way]).start()
                proj[...] += project(sources[0])
                for h in range(2):
                    for way in range(2):
                        ag_copy(it, way, h, 1, t, sources[way]).start()
                proj[...] += project(sources[1])
                for way in range(2):
                    for h in range(2):
                        ag_copy(it, way, h, 1, t - 1, between[way]).wait_recv()
                    proj[...] += project(between[way])
            between = (at_z(half_n - 1), at_z(n - half_n + 1))
            for way in range(2):
                for h in range(2):
                    ag_copy(it, way, h, 1, stops - 1, between[way]).wait_recv()
                proj[...] += project(between[way])
            for way in range(2):
                ag_copy(it, way, way, 0, stops - 1, far).wait_recv()
            proj[...] += project(far)

        return 0

    lax.fori_loop(0, ITERS, local_step, 0)

    own_three = jnp.concatenate([own[0], own[1]], axis=0)
    delta_in = own_three - own_zero
    out_cols = pl.ds(pl.multiple_of(z * width_out, 128), width_out)
    head_cols = head_ref[:, out_cols].astype(jnp.float32)
    delta_out = -learn_rate * mm(inner_sum[...], head_cols, NN, HIGH)
    delta = jnp.concatenate([delta_in, delta_out], axis=1)
    sums = jnp.sum(delta * delta, axis=0, keepdims=True)
    lanes = sums[:, :128]
    for j in range(1, width // 128):
        lanes = lanes + sums[:, j * 128 : (j + 1) * 128]
    squares = jnp.sum(lanes, axis=1, keepdims=True)
    weight = w_ref[0].astype(jnp.float32)

    mine = lax.broadcasted_iota(jnp.int32, (1, 128), 1) == client
    ends = jnp.concatenate(
        [jnp.where(mine, squares, 0.0), jnp.where(mine, weight, 0.0)], axis=1
    )
    for r in range(rank):
        row_out[r] = jnp.concatenate([delta[r : r + 1], ends], axis=1)

    def ro_copy(k, to_core, from_core):
        return pltpu.make_async_remote_copy(
            src_ref=row_out.at[at_chip(k)],
            dst_ref=row_in.at[client],
            send_sem=ro_send.at[k, to_core],
            recv_sem=ro_recv.at[k, from_core],
            device_id={"client": at_chip(k) * CORES + to_core},
            device_id_type=MESH,
        )

    for k in range(1, chips):
        for to_core in range(CORES):
            ro_copy(k, to_core, core).start()
    ro_copy(0, 1 - core, core).start()
    row_in[client] = row_out[chip]
    for k in range(1, chips):
        for from_core in range(CORES):
            ro_copy(k, from_core, from_core).wait_recv()
    ro_copy(0, 1 - core, 1 - core).wait_recv()
    ends = row_in[0][:, width:]
    for c in range(1, clients):
        ends = ends + row_in[c][:, width:]

    z_start(1, ends[:, :128])
    for piece in pieces[4:]:
        piece.wait()
    noise = jnp.concatenate(
        [nin_ref[pl.ds(chip, 1), :], nout_ref[pl.ds(chip, 1), :]], axis=1
    )
    weights = ends[:, 128:]
    wsum = jnp.sum(weights, axis=1, keepdims=True)
    scales = weights * jnp.minimum(1.0, clip_bound / jnp.sqrt(z_finish(1) + 1e-06))
    row = scales[:, :1] * row_in[0][:, :width]
    for c in range(1, clients):
        row = row + scales[:, c : c + 1] * row_in[c][:, :width]
    row_done[chip] = (row + noise_mult * clip_bound * noise) * out_scale / wsum

    def rd_copy(k):
        return pltpu.make_async_remote_copy(
            src_ref=row_done.at[chip],
            dst_ref=row_done.at[chip],
            send_sem=rd_send.at[k],
            recv_sem=rd_recv.at[k],
            device_id={"client": at_chip(k) * CORES + core},
            device_id_type=MESH,
        )

    for k in range(1, chips):
        rd_copy(k).start()

    def drain_step(it, _):
        for way in range(2):
            for e in range(stops):
                for h in range(2):
                    if long(way, h) or e > 0:
                        rs_copy(it, way, h, 0, e, z).wait_send()
                    rs_copy(it, way, h, 1, e, z).wait_send()
                if way == 0 or e < stops - 1:
                    pt_copy(it, way, 0, e, z).wait_send()
                pt_copy(it, way, 1, e, z).wait_send()

            @pl.when(it < ITERS - 1)
            def _():
                for e in range(stops):
                    for h in range(2):
                        if long(way, h) or e < stops - 1:
                            ag_copy(it, way, h, 0, e, z).wait_send()
                        ag_copy(it, way, h, 1, e, z).wait_send()

        return 0

    lax.fori_loop(0, ITERS, drain_step, 0)

    for k in range(1, chips):
        for to_core in range(CORES):
            ro_copy(k, to_core, core).wait_send()
    ro_copy(0, 1 - core, core).wait_send()
    for k in range(1, chips):
        rd_copy(k).wait()
    for r in range(rank):
        row = row_done[r]
        oin_ref[r : r + 1, :] = row[:, :width_in]
        oout_ref[r : r + 1, :] = row[:, width_in:]


def on_device(
    n,
    clients,
    hidden,
    frozen_residual,
    head,
    global_input_factor,
    global_output_factor,
    counts,
    weights,
    input_privacy_noise,
    output_privacy_noise,
):
    tokens, hidden_units = hidden.shape[1:]
    nout = head.shape[1]
    rank, model_width = global_output_factor.shape
    width_in = input_privacy_noise.shape[1]
    width_out = output_privacy_noise.shape[1]
    half = rank // 2
    stops = n // 4
    chips = clients // CORES
    width = width_in + width_out
    out_scale = math.sqrt(rank * (hidden_units + model_width)) / clip_bound
    f32 = jnp.float32
    dma = pltpu.SemaphoreType.DMA
    hbm = pl.BlockSpec(memory_space=pltpu.HBM)
    vmem = pl.BlockSpec(memory_space=pltpu.VMEM)
    smem = pl.BlockSpec(memory_space=pltpu.SMEM)
    return pl.pallas_call(
        functools.partial(kernel, n, clients, out_scale),
        out_shape=(
            jax.ShapeDtypeStruct((rank, width_in), f32),
            jax.ShapeDtypeStruct((rank, width_out), f32),
        ),
        in_specs=[
            hbm, hbm, hbm, hbm, hbm, smem, smem, hbm, hbm
        ],
        out_specs=(vmem, vmem),
        scratch_shapes=[
            pltpu.VMEM((nout, tokens), jnp.bfloat16),
            pltpu.VMEM((nout, model_width), jnp.bfloat16),
            pltpu.VMEM((rank, hidden_units), jnp.bfloat16),
            pltpu.VMEM((rank, model_width), jnp.bfloat16),
            pltpu.VMEM((rank, width_in), f32),
            pltpu.VMEM((rank, width_out), f32),
            pltpu.VMEM((n, tokens, width_in), jnp.bfloat16),
            pltpu.VMEM((nout, nout), f32),
            pltpu.VMEM((rank, nout), f32),
            pltpu.VMEM((nout, rank), f32),
            pltpu.VMEM((rank, nout), f32),
            pltpu.VMEM((1, tokens), f32),
            pltpu.VMEM((1, tokens), f32),
            pltpu.VMEM((tokens, rank), f32),
            pltpu.VMEM((rank, tokens), jnp.bfloat16),
            pltpu.VMEM((rank, rank), f32),
            pltpu.VMEM((rank, tokens), f32),
            pltpu.VMEM((ITERS, n, 2, half, width_in), f32),
            pltpu.VMEM((ITERS, 2, 2, 2, stops, half, width_in), f32),
            pltpu.VMEM((ITERS - 1, n, 2, half, width_in), f32),
            pltpu.VMEM((2, half, width_in), f32),
            pltpu.VMEM((ITERS, n, half, 128), f32),
            pltpu.VMEM((2, n, 1, 128), f32),
            pltpu.VMEM((rank, 1, width + 256), f32),
            pltpu.VMEM((clients, 1, width + 256), f32),
            pltpu.VMEM((rank, 1, width), f32),
            dma((6,)),
            dma((n,)),
            dma((ITERS, 2, 2, 2, stops)),
            dma((ITERS, 2, 2, 2, stops)),
            dma((ITERS - 1, 2, 2, 2, stops)),
            dma((ITERS - 1, 2, 2, 2, stops)),
            dma((ITERS, 2, 2, stops)),
            dma((ITERS, 2, 2, stops)),
            dma((2, n)),
            dma((2, n)),
            dma((chips, CORES)),
            dma((chips, CORES)),
            dma((chips,)),
            dma((chips,)),
        ],
        compiler_params=pltpu.CompilerParams(
            collective_id=0, has_side_effects=True, vmem_limit_bytes=63 * 1024 * 1024
        ),
    )(
        hidden,
        frozen_residual[0].T,
        head[0],
        global_input_factor,
        global_output_factor,
        counts,
        weights,
        input_privacy_noise,
        output_privacy_noise,
    )


def solution(mesh):
    in_specs = (
        P("client", "dp", None),
        P("client", "dp", None),
        P("client", None, None),
        P(),
        P(),
        P("client", "dp"),
        P("client"),
        P(None, "dp"),
        P(None, "dp"),
    )
    out_specs = (P(None, "dp"), P(None, "dp"))
    body = functools.partial(on_device, mesh.shape["dp"], mesh.shape["client"])
    return jax.shard_map(
        body, mesh=mesh, in_specs=in_specs, out_specs=out_specs, check_vma=False
    )
```

time: 191 us -> 143 us (0.75)
  Pallas kernels: 180 us -> 138 us
  local copies, waits for them, and re-layouts: 8.59 us -> 2.77 us
    pallas_call x1, Pallas kernels: 180 us -> 138 us  [on_device(): pl.pallas_call(functools.partial(kernel, n, clients, out_scale), out_shap...]
    unnamed x15 -> x2, local copies, waits for them, and re-layouts: 8.59 us -> 2.77 us
where the time goes in v2:
time: 143 us; the launch traced here: 142 us
  Pallas kernels  138 us (97%)
  local copies, waits for them, and re-layouts  2.77 us (2%)
  between operations  1.93 us (1%)
    pallas_call x1, Pallas kernels, on_device(): pl.pallas_call(functools.partial(kernel, n, clients, out_scale), out_shap...  138 us

profile of v2, /device:TPU:1, one launch (start us, length us, event | category | flops | bytes accessed | tf_op | source)
XLA Modules:
  0.0 142.3 jit_solution(13266876820817749816)
XLA Ops:
  1.9 137.6 %shard_map.104 = (f32[16,896]{1,0:T(8,128)}, f32[16,256]{1,0:T(8,128)}) custom-call(bf16[1,128,14336]{2,1,0:T(8,128)(2,1)} %hid_ref.1, bf16[64,128]{1,0:T(8,128)(2,1)} %bitcast.5, bf16[64,4096]{1,0:T(8,128)(2,1)} %bitcast.4, bf16[16,14336]{1,0:T(8,128)(2,1)} %a0_hbm.1, bf16[16,4096]{1,0:T(8,128)(2,1)} %b0_hbm.1, s32[1,1]{1,0:T(1,128)S(6)} %copy.13.cnt_ref, ...), custom_call_target="tpu_custom_call" | custom-call | tf_op jit(solution)/shard_map/pallas_call | solution.py:509
  139.6 1.4 %copy.15 = f32[16,896]{1,0:T(8,128)} copy(f32[16,896]{1,0:T(8,128)} %get-tuple-element.4) | data formatting | bytes 114688
  141.0 1.3 copy.16

commit v3 on v2

--- a/solution.py
+++ b/solution.py
@@ -14,6 +14,9 @@
 learn_rate = 0.1
 clip_bound = 0.001
 noise_mult = 0.1
+
+PARENT = {8: 6, 7: 6, 6: 4, 5: 4, 4: 2, 3: 2, 2: 0, 1: 0}
+CHILDREN = {p: [k for k in PARENT if PARENT[k] == p] for p in range(9)}
 
 MESH = pl.DeviceIdType.MESH
 HIGH = lax.Precision.HIGHEST
@@ -64,7 +67,9 @@
     slot,
     a_all,
     own,
-    part,
+    inner_out,
+    inner_in,
+    inner_all,
     spread,
     row_out,
     row_in,
@@ -75,8 +80,10 @@
     rs_recv,
     ag_send,
     ag_recv,
-    pt_send,
-    pt_recv,
+    ir_send,
+    ir_recv,
+    is_send,
+    is_recv,
     sc_send,
     sc_recv,
     ro_send,
@@ -85,7 +92,6 @@
     rd_recv,
 ):
     half_n = n // 2
-    stops = half_n // 2
     chips = clients // CORES
     rank, width_in = nin_ref.shape
     width_out = nout_ref.shape[1]
@@ -98,16 +104,19 @@
     client = lax.axis_index("client")
     chip = lax.div(client, CORES)
     core = lax.rem(client, CORES)
-    ring = (
-        (lax.rem(z + n - 2, n), lax.rem(z + 2, n)),
-        (lax.rem(z + n - 1, n), lax.rem(z + 1, n)),
-    )
-
     def at_z(k):
         return lax.rem(z + k, n)
 
     def at_chip(k):
         return lax.rem(chip + k, chips)
+
+    barrier = pltpu.get_barrier_semaphore()
+    for k in range(1, n):
+        pl.semaphore_signal(barrier, inc=1, device_id={"dp": at_z(k)}, device_id_type=MESH)
+    for k in range(1, clients):
+        pl.semaphore_signal(
+            barrier, inc=1, device_id={"client": lax.rem(client + k, clients)}, device_id_type=MESH
+        )
 
     def load(j):
         return pltpu.make_async_copy(
@@ -134,27 +143,6 @@
     for piece in pieces[4:]:
         piece.start()
 
-    barrier = pltpu.get_barrier_semaphore()
-    for k in range(1, n):
-        pl.semaphore_signal(barrier, inc=1, device_id={"dp": at_z(k)}, device_id_type=MESH)
-    for k in range(1, clients):
-        pl.semaphore_signal(
-            barrier, inc=1, device_id={"client": lax.rem(client + k, clients)}, device_id_type=MESH
-        )
-
-    for piece in pieces[:3]:
-        piece.wait()
-    head = head_ref[...]
-    gram[...] = mm(head, head, NT)
-    mixed[...] = mm(b0_ref[...], head, NT)
-    mixed_t[...] = mm(head, b0_ref[...], NT)
-    inner_sum[...] = jnp.zeros_like(inner_sum)
-
-    def from_mixed():
-        square[...] = mm(mixed[...], mixed[...], NT, HIGH)
-        base_in[...] = mm(mixed[...], res_ref[...].astype(jnp.float32), NN, HIGH)
-
-    from_mixed()
     lane = lax.broadcasted_iota(jnp.int32, (1, tokens), 1)
     live = cnt_ref[0, 0]
 
@@ -185,6 +173,19 @@
 
     z_start(0, jnp.full((1, 128), live.astype(jnp.float32), jnp.float32))
 
+    for piece in pieces[:3]:
+        piece.wait()
+    head = head_ref[...]
+    gram[...] = mm(head, head, NT)
+    mixed[...] = mm(b0_ref[...], head, NT)
+    mixed_t[...] = mm(head, b0_ref[...], NT)
+    inner_sum[...] = jnp.zeros_like(inner_sum)
+
+    def from_mixed():
+        square[...] = mm(mixed[...], mixed[...], NT, HIGH)
+        base_in[...] = mm(mixed[...], res_ref[...].astype(jnp.float32), NN, HIGH)
+
+    from_mixed()
     pieces[3].wait()
     proj[...] = jnp.zeros_like(proj)
 
@@ -203,39 +204,56 @@
     mask[...] = (lane < live).astype(jnp.float32)
     tokens_live[...] = z_finish(0)
 
-    def rs_copy(it, way, h, odd, e, owner):
+    def toward(way, k):
+        return at_z(n - k) if way == 0 else at_z(k)
+
+    def rs_copy(it, way, h, k, owner):
         return pltpu.make_async_remote_copy(
             src_ref=grad.at[it, owner, h],
-            dst_ref=slot.at[it, way, h, odd, e],
-            send_sem=rs_send.at[it, way, h, odd, e],
-            recv_sem=rs_recv.at[it, way, h, odd, e],
-            device_id={"dp": ring[odd][way]},
+            dst_ref=slot.at[it, way, h, k - 1],
+            send_sem=rs_send.at[it, way, h, k - 1],
+            recv_sem=rs_recv.at[it, way, h, k - 1],
+            device_id={"dp": toward(way, k - PARENT[k])},
             device_id_type=MESH,
         )
 
-    def ag_copy(it, way, h, odd, t, owner):
+    def ag_copy(it, way, h, k, owner):
         return pltpu.make_async_remote_copy(
             src_ref=a_all.at[it, owner, h],
             dst_ref=a_all.at[it, owner, h],
-            send_sem=ag_send.at[it, way, h, odd, t],
-            recv_sem=ag_recv.at[it, way, h, odd, t],
-            device_id={"dp": ring[odd][way]},
+            send_sem=ag_send.at[it, way, h, k - 1],
+            recv_sem=ag_recv.at[it, way, h, k - 1],
+            device_id={"dp": toward(way, k - PARENT[k])},
             device_id_type=MESH,
         )
 
-    def pt_copy(it, way, odd, t, owner):
+    def row_copy(it, k):
         return pltpu.make_async_remote_copy(
-            src_ref=part.at[it, owner],
-            dst_ref=part.at[it, owner],
-            send_sem=pt_send.at[it, way, odd, t],
-            recv_sem=pt_recv.at[it, way, odd, t],
-            device_id={"dp": ring[odd][way]},
+            src_ref=inner_out.at[it, at_z(k)],
+            dst_ref=inner_in.at[it, z],
+            send_sem=ir_send.at[it, k],
+            recv_sem=ir_recv.at[it, k],
+            device_id={"dp": at_z(k)},
+            device_id_type=MESH,
+        )
+
+    def sum_copy(it, k):
+        return pltpu.make_async_remote_copy(
+            src_ref=inner_all.at[it, z],
+            dst_ref=inner_all.at[it, z],
+            send_sem=is_send.at[it, k],
+            recv_sem=is_recv.at[it, k],
+            device_id={"dp": at_z(k)},
             device_id_type=MESH,
         )
 
     def long(way, h):
         return way == h
 
+    def reaches(way, h, k):
+        return k < half_n or long(way, h)
+
+    chains = ((0, 0), (1, 1), (0, 1), (1, 0))
     far = at_z(half_n)
 
     def local_step(it, _):
@@ -248,125 +266,160 @@
             for h in range(2):
                 grad[it, owner, h] = value[h * half : (h + 1) * half]
 
-        def beside(k):
-            return at_z(n - k), at_z(k)
-
         def local_both(k):
-            for owner in beside(k):
-                local(owner)
-
-        def send_odd(e):
-            owners = beside(half_n - 1 - 2 * e)
-            for h in range(2):
-                for way in range(2):
-                    rs_copy(it, way, h, 1, e, owners[way]).start()
+            for way in range(2):
+                local(toward(way, k))
+
+        def send_raw(k, h):
+            for way in range(2):
+                if reaches(way, h, k):
+                    rs_copy(it, way, h, k, toward(way, k)).start()
+
+        def gather_terms(way, h, k, owner):
+            total = grad[it, owner, h]
+            for child in reversed(CHILDREN[k]):
+                if reaches(way, h, child):
+                    rs_copy(it, way, h, child, owner).wait_recv()
+                    total = total + slot[it, way, h, child - 1]
+            return total
+
+        def send_on(way, h, k):
+            owner = toward(way, k)
+            grad[it, owner, h] = gather_terms(way, h, k, owner)
+            rs_copy(it, way, h, k, owner).start()
 
         local(far)
-        for way in range(2):
-            rs_copy(it, way, way, 0, 0, far).start()
-        local_both(half_n - 1)
-        send_odd(0)
-        local_both(half_n - 2)
-        local_both(half_n - 3)
-        send_odd(1)
-
+        send_raw(8, 0)
+        local_both(7)
+        send_raw(7, 0)
+        local_both(6)
+        local_both(5)
+        send_raw(5, 0)
         proj_t = proj[...].T
         resid = res_ref[...].astype(jnp.float32) + mm(mixed_t[...], proj_t, NN, HIGH)
         inner = mm(proj_t, resid * weighted, NT, HIGH)
-        part[it, z] = jnp.concatenate([inner[:half], inner[half:]], axis=1)
-        for odd in range(2):
+        send_raw(8, 1)
+        send_raw(7, 1)
+        send_raw(5, 1)
+        wide = jnp.concatenate([inner, jnp.zeros_like(inner)], axis=1)
+        for r in range(rank):
+            inner_out[it, r] = wide[r : r + 1]
+        inner_in[it, z] = inner_out[it, z]
+        for k in range(1, n):
+            row_copy(it, k).start()
+        for k in (6, 4, 2):
             for way in range(2):
-                pt_copy(it, way, odd, 0, z).start()
-
-        for e in range(1, stops):
-            owners = beside(half_n - 2 * e)
-            for h in range(2):
-                for way in range(2):
-                    rs_copy(it, way, h, 1, e - 1, owners[way]).wait_recv()
-                    total = grad[it, owners[way], h] + slot[it, way, h, 1, e - 1]
-                    if long(way, h) or e > 1:
-                        rs_copy(it, way, h, 0, e - 1, owners[way]).wait_recv()
-                        total = total + slot[it, way, h, 0, e - 1]
-                    grad[it, owners[way], h] = total
-                    rs_copy(it, way, h, 0, e, owners[way]).start()
-            if e < stops - 1:
-                local_both(half_n - 2 * e - 2)
-                local_both(half_n - 2 * e - 3)
-                send_odd(e + 1)
+                send_on(way, 0, k)
+            if k > 2:
+                local_both(k - 2)
+                local_both(k - 3)
+                send_raw(k - 3, 0)
             else:
                 local(z)
             for way in range(2):
-                source = at_z(2 * e) if way == 0 else at_z(n - 2 * e)
-                pt_copy(it, way, 0, e - 1, source).wait_recv()
-                if way == 0 or e < stops - 1:
-                    pt_copy(it, way, 0, e, source).start()
-                pt_copy(it, way, 1, e, source).start()
-                pt_copy(it, way, 1, e - 1, source).wait_recv()
+                send_on(way, 1, k)
+            if k > 2:
+                send_raw(k - 3, 1)
+            if k == 4:
+                for j in range(1, n):
+                    row_copy(it, j).wait_recv()
+                total = inner_in[it, 0]
+                for j in range(1, n):
+                    total = total + inner_in[it, j]
+                inner_all[it, z] = total
+                for j in range(1, n):
+                    sum_copy(it, j).start()
         for h in range(2):
             total = grad[it, z, h]
-            for odd in (1, 0):
-                for way in range(2):
-                    rs_copy(it, way, h, odd, stops - 1, z).wait_recv()
-                    total = total + slot[it, way, h, odd, stops - 1]
+            for way in range(2):
+                for child in CHILDREN[0]:
+                    rs_copy(it, way, h, child, z).wait_recv()
+                    total = total + slot[it, way, h, child - 1]
             own[h] = own[h] - learn_rate * total
 
             @pl.when(it < ITERS - 1)
             def _():
                 a_all[it, z, h] = own[h]
                 for way in range(2):
-                    ag_copy(it, way, h, 0, 0, z).start()
+                    ag_copy(it, way, h, 2, z).start()
+
+        def inner_total():
+            for k in range(1, n):
+                sum_copy(it, k).wait_recv()
+            rows = [inner_all[it, r][:, :nout] for r in range(rank)]
+            return jnp.concatenate(rows, axis=0)
+
+        @pl.when(it == ITERS - 1)
+        def _():
+            inner_sum[...] += inner_total()
 
         @pl.when(it < ITERS - 1)
         def _():
-            for h in range(2):
-                for way in range(2):
-                    ag_copy(it, way, h, 1, 0, z).start()
-
-        pt_copy(it, 0, 0, stops - 1, far).wait_recv()
-        for way in range(2):
-            pt_copy(it, way, 1, stops - 1, far).wait_recv()
-        tile = part[it, 0]
-        for j in range(1, n):
-            tile = tile + part[it, j]
-        step_inner = jnp.concatenate([tile[:, :nout], tile[:, nout:]], axis=0)
-        inner_sum[...] += step_inner
-
-        @pl.when(it < ITERS - 1)
-        def _():
-            mixed[...] = mixed[...] - learn_rate * mm(step_inner, gram[...], NN, HIGH)
-            mixed_t[...] = mixed_t[...] - learn_rate * mm(gram[...], step_inner, NT, HIGH)
-            from_mixed()
-
             def project(owner):
                 rows = jnp.concatenate([a_all[it, owner, 0], a_all[it, owner, 1]], axis=0)
                 return mm(hv[owner], rows.astype(jnp.bfloat16), NT)
 
+            def use(k):
+                for way in range(2):
+                    proj[...] += project(toward(1 - way, k))
+
+            def arrive(k, h):
+                for way in range(2):
+                    if reaches(way, h, k):
+                        ag_copy(it, way, h, k, toward(1 - way, k)).wait_recv()
+
+            def pass_on(parent, k, h):
+                for way in range(2):
+                    if reaches(way, h, k):
+                        ag_copy(it, way, h, k, toward(1 - way, parent)).start()
+
+            pass_on(0, 1, 0)
             proj[...] = project(z)
-
-            for t in range(1, stops):
-                sources = (at_z(2 * t), at_z(n - 2 * t))
-                between = (at_z(2 * t - 1), at_z(n - 2 * t + 1))
-                for h in range(2):
-                    for way in range(2):
-                        ag_copy(it, way, h, 0, t - 1, sources[way]).wait_recv()
-                        if long(way, h) or t < stops - 1:
-                            ag_copy(it, way, h, 0, t, sources[way]).start()
-                proj[...] += project(sources[0])
-                for h in range(2):
-                    for way in range(2):
-                        ag_copy(it, way, h, 1, t, sources[way]).start()
-                proj[...] += project(sources[1])
-                for way in range(2):
-                    for h in range(2):
-                        ag_copy(it, way, h, 1, t - 1, between[way]).wait_recv()
-                    proj[...] += project(between[way])
-            between = (at_z(half_n - 1), at_z(n - half_n + 1))
-            for way in range(2):
-                for h in range(2):
-                    ag_copy(it, way, h, 1, stops - 1, between[way]).wait_recv()
-                proj[...] += project(between[way])
-            for way in range(2):
-                ag_copy(it, way, way, 0, stops - 1, far).wait_recv()
+            pass_on(0, 1, 1)
+
+            arrive(2, 0)
+            pass_on(2, 4, 0)
+            step_inner = inner_total()
+            inner_sum[...] += step_inner
+            pass_on(2, 3, 0)
+            arrive(2, 1)
+            pass_on(2, 4, 1)
+            use(2)
+            pass_on(2, 3, 1)
+            arrive(1, 0)
+            arrive(1, 1)
+            use(1)
+
+            arrive(4, 0)
+            pass_on(4, 6, 0)
+            mixed[...] = mixed[...] - learn_rate * mm(step_inner, gram[...], NN, HIGH)
+            mixed_t[...] = mixed_t[...] - learn_rate * mm(gram[...], step_inner, NT, HIGH)
+            pass_on(4, 5, 0)
+            arrive(4, 1)
+            pass_on(4, 6, 1)
+            use(4)
+            pass_on(4, 5, 1)
+            arrive(3, 0)
+            arrive(3, 1)
+            use(3)
+
+            arrive(6, 0)
+            pass_on(6, 8, 0)
+            pass_on(6, 7, 0)
+            from_mixed()
+            arrive(6, 1)
+            pass_on(6, 8, 1)
+            pass_on(6, 7, 1)
+            use(6)
+            arrive(5, 0)
+            arrive(5, 1)
+            use(5)
+
+            arrive(7, 0)
+            arrive(7, 1)
+            use(7)
+            arrive(8, 0)
+            arrive(8, 1)
             proj[...] += project(far)
 
         return 0
@@ -444,23 +497,20 @@
         rd_copy(k).start()
 
     def drain_step(it, _):
-        for way in range(2):
-            for e in range(stops):
-                for h in range(2):
-                    if long(way, h) or e > 0:
-                        rs_copy(it, way, h, 0, e, z).wait_send()
-                    rs_copy(it, way, h, 1, e, z).wait_send()
-                if way == 0 or e < stops - 1:
-                    pt_copy(it, way, 0, e, z).wait_send()
-                pt_copy(it, way, 1, e, z).wait_send()
-
-            @pl.when(it < ITERS - 1)
-            def _():
-                for e in range(stops):
-                    for h in range(2):
-                        if long(way, h) or e < stops - 1:
-                            ag_copy(it, way, h, 0, e, z).wait_send()
-                        ag_copy(it, way, h, 1, e, z).wait_send()
+        for way, h in chains:
+            for k in PARENT:
+                if reaches(way, h, k):
+                    rs_copy(it, way, h, k, z).wait_send()
+        for k in range(1, n):
+            row_copy(it, k).wait_send()
+            sum_copy(it, k).wait_send()
+
+        @pl.when(it < ITERS - 1)
+        def _():
+            for way, h in chains:
+                for k in PARENT:
+                    if reaches(way, h, k):
+                        ag_copy(it, way, h, k, z).wait_send()
 
         return 0
 
@@ -497,7 +547,7 @@
     width_in = input_privacy_noise.shape[1]
     width_out = output_privacy_noise.shape[1]
     half = rank // 2
-    stops = n // 4
+    half_n = n // 2
     chips = clients // CORES
     width = width_in + width_out
     out_scale = math.sqrt(rank * (hidden_units + model_width)) / clip_bound
@@ -535,22 +585,26 @@
             pltpu.VMEM((rank, rank), f32),
             pltpu.VMEM((rank, tokens), f32),
             pltpu.VMEM((ITERS, n, 2, half, width_in), f32),
-            pltpu.VMEM((ITERS, 2, 2, 2, stops, half, width_in), f32),
+            pltpu.VMEM((ITERS, 2, 2, half_n, half, width_in), f32),
             pltpu.VMEM((ITERS - 1, n, 2, half, width_in), f32),
             pltpu.VMEM((2, half, width_in), f32),
-            pltpu.VMEM((ITERS, n, half, 128), f32),
+            pltpu.VMEM((ITERS, n, 1, 128), f32),
+            pltpu.VMEM((ITERS, n, 1, 128), f32),
+            pltpu.VMEM((ITERS, n, 1, 128), f32),
             pltpu.VMEM((2, n, 1, 128), f32),
             pltpu.VMEM((rank, 1, width + 256), f32),
             pltpu.VMEM((clients, 1, width + 256), f32),
             pltpu.VMEM((rank, 1, width), f32),
             dma((6,)),
             dma((n,)),
-            dma((ITERS, 2, 2, 2, stops)),
-            dma((ITERS, 2, 2, 2, stops)),
-            dma((ITERS - 1, 2, 2, 2, stops)),
-            dma((ITERS - 1, 2, 2, 2, stops)),
-            dma((ITERS, 2, 2, stops)),
-            dma((ITERS, 2, 2, stops)),
+            dma((ITERS, 2, 2, half_n)),
+            dma((ITERS, 2, 2, half_n)),
+            dma((ITERS - 1, 2, 2, half_n)),
+            dma((ITERS - 1, 2, 2, half_n)),
+            dma((ITERS, n)),
+            dma((ITERS, n)),
+            dma((ITERS, n)),
+            dma((ITERS, n)),
             dma((2, n)),
             dma((2, n)),
             dma((chips, CORES)),

time: 143 us -> 144 us (level)
    pallas_call x1, Pallas kernels: 138 us -> 139 us  [on_device(): pl.pallas_call(functools.partial(kernel, n, clients, out_scale), out_shap...]
where the time goes in v3:
time: 144 us
  Pallas kernels  139 us (97%)
  local copies, waits for them, and re-layouts  2.77 us (2%)
  between operations  1.93 us (1%)
    pallas_call x1, Pallas kernels, on_device(): pl.pallas_call(functools.partial(kernel, n, clients, out_scale), out_shap...  139 us

profile of v3, /device:TPU:1, one launch (start us, length us, event | category | flops | bytes accessed | tf_op | source)
XLA Modules:
  0.0 144.1 jit_solution(462482289110352724)
XLA Ops:
  1.9 139.4 %shard_map.104 = (f32[16,896]{1,0:T(8,128)}, f32[16,256]{1,0:T(8,128)}) custom-call(bf16[1,128,14336]{2,1,0:T(8,128)(2,1)} %hid_ref.1, bf16[64,128]{1,0:T(8,128)(2,1)} %bitcast.5, bf16[64,4096]{1,0:T(8,128)(2,1)} %bitcast.4, bf16[16,14336]{1,0:T(8,128)(2,1)} %a0_hbm.1, bf16[16,4096]{1,0:T(8,128)(2,1)} %b0_hbm.1, s32[1,1]{1,0:T(1,128)S(6)} %copy.13.cnt_ref, ...), custom_call_target="tpu_custom_call" | custom-call | tf_op jit(solution)/shard_map/pallas_call | solution.py:559
  141.4 1.4 %copy.15 = f32[16,896]{1,0:T(8,128)} copy(f32[16,896]{1,0:T(8,128)} %get-tuple-element.4) | data formatting | bytes 114688
  142.8 1.3 copy.16

commit v4 on v3

--- a/solution.py
+++ b/solution.py
@@ -10,6 +10,8 @@
 
 ITERS = 3
 CORES = 2
+BLOCK = 4
+VMEM_BYTES = 63 * 1024 * 1024
 
 learn_rate = 0.1
 clip_bound = 0.001
@@ -44,8 +46,7 @@
     w_ref,
     nin_hbm,
     nout_hbm,
-    oin_ref,
-    oout_ref,
+    out_ref,
     res_ref,
     head_ref,
     a0_ref,
@@ -69,7 +70,6 @@
     own,
     inner_out,
     inner_in,
-    inner_all,
     spread,
     row_out,
     row_in,
@@ -80,10 +80,8 @@
     rs_recv,
     ag_send,
     ag_recv,
-    ir_send,
-    ir_recv,
-    is_send,
-    is_recv,
+    in_send,
+    in_recv,
     sc_send,
     sc_recv,
     ro_send,
@@ -104,19 +102,13 @@
     client = lax.axis_index("client")
     chip = lax.div(client, CORES)
     core = lax.rem(client, CORES)
+    corner = lax.div(z, BLOCK) * BLOCK
+
     def at_z(k):
         return lax.rem(z + k, n)
 
     def at_chip(k):
         return lax.rem(chip + k, chips)
-
-    barrier = pltpu.get_barrier_semaphore()
-    for k in range(1, n):
-        pl.semaphore_signal(barrier, inc=1, device_id={"dp": at_z(k)}, device_id_type=MESH)
-    for k in range(1, clients):
-        pl.semaphore_signal(
-            barrier, inc=1, device_id={"client": lax.rem(client + k, clients)}, device_id_type=MESH
-        )
 
     def load(j):
         return pltpu.make_async_copy(
@@ -143,6 +135,28 @@
     for piece in pieces[4:]:
         piece.start()
 
+    barrier = pltpu.get_barrier_semaphore()
+    for k in range(1, n):
+        pl.semaphore_signal(barrier, inc=1, device_id={"dp": at_z(k)}, device_id_type=MESH)
+    for k in range(1, clients):
+        pl.semaphore_signal(
+            barrier, inc=1, device_id={"client": lax.rem(client + k, clients)}, device_id_type=MESH
+        )
+
+    for piece in pieces[:3]:
+        piece.wait()
+    head = head_ref[...]
+    gram[...] = mm(head, head, NT)
+    mixed[...] = mm(b0_ref[...], head, NT)
+    mixed_t[...] = mm(head, b0_ref[...], NT)
+    inner_sum[...] = jnp.zeros_like(inner_sum)
+
+    def from_mixed():
+        square[...] = mm(mixed[...], mixed[...], NT, HIGH)
+        base_in[...] = mm(mixed[...], res_ref[...].astype(jnp.float32), NN, HIGH)
+
+    from_mixed()
+
     lane = lax.broadcasted_iota(jnp.int32, (1, tokens), 1)
     live = cnt_ref[0, 0]
 
@@ -173,19 +187,6 @@
 
     z_start(0, jnp.full((1, 128), live.astype(jnp.float32), jnp.float32))
 
-    for piece in pieces[:3]:
-        piece.wait()
-    head = head_ref[...]
-    gram[...] = mm(head, head, NT)
-    mixed[...] = mm(b0_ref[...], head, NT)
-    mixed_t[...] = mm(head, b0_ref[...], NT)
-    inner_sum[...] = jnp.zeros_like(inner_sum)
-
-    def from_mixed():
-        square[...] = mm(mixed[...], mixed[...], NT, HIGH)
-        base_in[...] = mm(mixed[...], res_ref[...].astype(jnp.float32), NN, HIGH)
-
-    from_mixed()
     pieces[3].wait()
     proj[...] = jnp.zeros_like(proj)
 
@@ -227,25 +228,28 @@
             device_id_type=MESH,
         )
 
-    def row_copy(it, k):
+    def inner_copy(it, stage, j):
+        peer = at_z(j * BLOCK) if stage == 0 else corner + lax.rem(z - corner + j, BLOCK)
         return pltpu.make_async_remote_copy(
-            src_ref=inner_out.at[it, at_z(k)],
-            dst_ref=inner_in.at[it, z],
-            send_sem=ir_send.at[it, k],
-            recv_sem=ir_recv.at[it, k],
-            device_id={"dp": at_z(k)},
+            src_ref=inner_out.at[it, stage],
+            dst_ref=inner_in.at[it, stage, j - 1],
+            send_sem=in_send.at[it, stage, j - 1],
+            recv_sem=in_recv.at[it, stage, j - 1],
+            device_id={"dp": peer},
             device_id_type=MESH,
         )
 
-    def sum_copy(it, k):
-        return pltpu.make_async_remote_copy(
-            src_ref=inner_all.at[it, z],
-            dst_ref=inner_all.at[it, z],
-            send_sem=is_send.at[it, k],
-            recv_sem=is_recv.at[it, k],
-            device_id={"dp": at_z(k)},
-            device_id_type=MESH,
-        )
+    def inner_start(it, stage, value):
+        inner_out[it, stage] = value
+        for j in range(1, BLOCK):
+            inner_copy(it, stage, j).start()
+
+    def inner_finish(it, stage):
+        total = inner_out[it, stage]
+        for j in range(1, BLOCK):
+            inner_copy(it, stage, j).wait_recv()
+            total = total + inner_in[it, stage, j - 1]
+        return total
 
     def long(way, h):
         return way == h
@@ -301,12 +305,7 @@
         send_raw(8, 1)
         send_raw(7, 1)
         send_raw(5, 1)
-        wide = jnp.concatenate([inner, jnp.zeros_like(inner)], axis=1)
-        for r in range(rank):
-            inner_out[it, r] = wide[r : r + 1]
-        inner_in[it, z] = inner_out[it, z]
-        for k in range(1, n):
-            row_copy(it, k).start()
+        inner_start(it, 0, jnp.concatenate([inner[:half], inner[half:]], axis=1))
         for k in (6, 4, 2):
             for way in range(2):
                 send_on(way, 0, k)
@@ -321,14 +320,7 @@
             if k > 2:
                 send_raw(k - 3, 1)
             if k == 4:
-                for j in range(1, n):
-                    row_copy(it, j).wait_recv()
-                total = inner_in[it, 0]
-                for j in range(1, n):
-                    total = total + inner_in[it, j]
-                inner_all[it, z] = total
-                for j in range(1, n):
-                    sum_copy(it, j).start()
+                inner_start(it, 1, inner_finish(it, 0))
         for h in range(2):
             total = grad[it, z, h]
             for way in range(2):
@@ -344,10 +336,8 @@
                     ag_copy(it, way, h, 2, z).start()
 
         def inner_total():
-            for k in range(1, n):
-                sum_copy(it, k).wait_recv()
-            rows = [inner_all[it, r][:, :nout] for r in range(rank)]
-            return jnp.concatenate(rows, axis=0)
+            tile = inner_finish(it, 1)
+            return jnp.concatenate([tile[:, :nout], tile[:, nout:]], axis=0)
 
         @pl.when(it == ITERS - 1)
         def _():
@@ -501,9 +491,9 @@
             for k in PARENT:
                 if reaches(way, h, k):
                     rs_copy(it, way, h, k, z).wait_send()
-        for k in range(1, n):
-            row_copy(it, k).wait_send()
-            sum_copy(it, k).wait_send()
+        for stage in range(2):
+            for j in range(1, BLOCK):
+                inner_copy(it, stage, j).wait_send()
 
         @pl.when(it < ITERS - 1)
         def _():
@@ -523,9 +513,20 @@
     for k in range(1, chips):
         rd_copy(k).wait()
     for r in range(rank):
-        row = row_done[r]
-        oin_ref[r : r + 1, :] = row[:, :width_in]
-        oout_ref[r : r + 1, :] = row[:, width_in:]
+        out_ref[r : r + 1, :] = row_done[r]
+
+
+def split(rows_ref, oin_ref, oout_ref, sem):
+    width_in = oin_ref.shape[1]
+    width_out = oout_ref.shape[1]
+    parts = (
+        pltpu.make_async_copy(rows_ref.at[:, pl.ds(0, width_in)], oin_ref, sem.at[0]),
+        pltpu.make_async_copy(rows_ref.at[:, pl.ds(width_in, width_out)], oout_ref, sem.at[1]),
+    )
+    for part in parts:
+        part.start()
+    for part in parts:
+        part.wait()
 
 
 def on_device(
@@ -556,16 +557,13 @@
     hbm = pl.BlockSpec(memory_space=pltpu.HBM)
     vmem = pl.BlockSpec(memory_space=pltpu.VMEM)
     smem = pl.BlockSpec(memory_space=pltpu.SMEM)
-    return pl.pallas_call(
+    rows = pl.pallas_call(
         functools.partial(kernel, n, clients, out_scale),
-        out_shape=(
-            jax.ShapeDtypeStruct((rank, width_in), f32),
-            jax.ShapeDtypeStruct((rank, width_out), f32),
-        ),
+        out_shape=jax.ShapeDtypeStruct((rank, width), f32),
         in_specs=[
             hbm, hbm, hbm, hbm, hbm, smem, smem, hbm, hbm
         ],
-        out_specs=(vmem, vmem),
+        out_specs=vmem,
         scratch_shapes=[
             pltpu.VMEM((nout, tokens), jnp.bfloat16),
             pltpu.VMEM((nout, model_width), jnp.bfloat16),
@@ -588,9 +586,8 @@
             pltpu.VMEM((ITERS, 2, 2, half_n, half, width_in), f32),
             pltpu.VMEM((ITERS - 1, n, 2, half, width_in), f32),
             pltpu.VMEM((2, half, width_in), f32),
-            pltpu.VMEM((ITERS, n, 1, 128), f32),
-            pltpu.VMEM((ITERS, n, 1, 128), f32),
-            pltpu.VMEM((ITERS, n, 1, 128), f32),
+            pltpu.VMEM((ITERS, 2, half, 128), f32),
+            pltpu.VMEM((ITERS, 2, BLOCK - 1, half, 128), f32),
             pltpu.VMEM((2, n, 1, 128), f32),
             pltpu.VMEM((rank, 1, width + 256), f32),
             pltpu.VMEM((clients, 1, width + 256), f32),
@@ -601,10 +598,8 @@
             dma((ITERS, 2, 2, half_n)),
             dma((ITERS - 1, 2, 2, half_n)),
             dma((ITERS - 1, 2, 2, half_n)),
-            dma((ITERS, n)),
-            dma((ITERS, n)),
-            dma((ITERS, n)),
-            dma((ITERS, n)),
+            dma((ITERS, 2, BLOCK - 1)),
+            dma((ITERS, 2, BLOCK - 1)),
             dma((2, n)),
             dma((2, n)),
             dma((chips, CORES)),
@@ -613,7 +608,7 @@
             dma((chips,)),
         ],
         compiler_params=pltpu.CompilerParams(
-            collective_id=0, has_side_effects=True, vmem_limit_bytes=63 * 1024 * 1024
+            collective_id=0, has_side_effects=True, vmem_limit_bytes=VMEM_BYTES
         ),
     )(
         hidden,
@@ -626,6 +621,17 @@
         input_privacy_noise,
         output_privacy_noise,
     )
+    return pl.pallas_call(
+        split,
+        out_shape=(
+            jax.ShapeDtypeStruct((rank, width_in), f32),
+            jax.ShapeDtypeStruct((rank, width_out), f32),
+        ),
+        in_specs=[hbm],
+        out_specs=(hbm, hbm),
+        scratch_shapes=[dma((2,))],
+        compiler_params=pltpu.CompilerParams(vmem_limit_bytes=VMEM_BYTES),
+    )(rows)
 
 
 def solution(mesh):

time: 144 us -> 144 us (level)
  Pallas kernels: 139 us -> 142 us
  local copies, waits for them, and re-layouts: 2.77 us -> 0 us
    pallas_call x0 -> x1, Pallas kernels: none -> 3.35 us  [on_device(): pl.pallas_call(split, out_shape=(jax.ShapeDtypeStruct((rank, width_in), f...]
    unnamed x2 -> x0, local copies, waits for them, and re-layouts: 2.77 us -> none
where the time goes in v4:
time: 144 us
  Pallas kernels  142 us (99%)
  between operations  1.93 us (1%)
    pallas_call x1, Pallas kernels, on_device(): pl.pallas_call(functools.partial(kernel, n, clients, out_scale), out_shap...  139 us
    pallas_call x1, Pallas kernels, on_device(): pl.pallas_call(split, out_shape=(jax.ShapeDtypeStruct((rank, width_in), f...  3.35 us

profile of v4, /device:TPU:1, one launch (start us, length us, event | category | flops | bytes accessed | tf_op | source)
XLA Modules:
  0.0 144.0 jit_solution(4589777851096274328)
XLA Ops:
  1.9 138.7 %shard_map.104.rows_ref = f32[16,1152]{1,0:T(8,128)} custom-call(bf16[1,128,14336]{2,1,0:T(8,128)(2,1)} %hid_ref.1, bf16[64,128]{1,0:T(8,128)(2,1)} %bitcast.5, bf16[64,4096]{1,0:T(8,128)(2,1)} %bitcast.4, bf16[16,14336]{1,0:T(8,128)(2,1)} %a0_hbm.1, bf16[16,4096]{1,0:T(8,128)(2,1)} %b0_hbm.1, s32[1,1]{1,0:T(1,128)S(6)} %copy.11.cnt_ref, s32[1]{0:T(128)S(6)} %copy.12.w_ref, ...), custom_call_target="tpu_custom_call" | custom-call | tf_op jit(solution)/shard_map/pallas_call | solution.py:560
  140.7 3.4 %shard_map.105 = (f32[16,896]{1,0:T(8,128)}, f32[16,256]{1,0:T(8,128)}) custom-call(f32[16,1152]{1,0:T(8,128)} %shard_map.104.rows_ref), custom_call_target="tpu_custom_call" | custom-call | tf_op jit(solution)/shard_map/pallas_call | solution.py:624

commit v5 on v4

--- a/solution.py
+++ b/solution.py
@@ -17,8 +17,10 @@
 clip_bound = 0.001
 noise_mult = 0.1
 
-PARENT = {8: 6, 7: 6, 6: 4, 5: 4, 4: 2, 3: 2, 2: 0, 1: 0}
+PARENT = {8: 6, 7: 6, 6: 3, 5: 3, 4: 3, 3: 0, 2: 0, 1: 0}
 CHILDREN = {p: [k for k in PARENT if PARENT[k] == p] for p in range(9)}
+LEAVES = {p: [k for k in CHILDREN[p] if not CHILDREN[k]] for p in CHILDREN}
+STOPS = [k for k in PARENT if CHILDREN[k]]
 
 MESH = pl.DeviceIdType.MESH
 HIGH = lax.Precision.HIGHEST
@@ -46,7 +48,8 @@
     w_ref,
     nin_hbm,
     nout_hbm,
-    out_ref,
+    oin_ref,
+    oout_ref,
     res_ref,
     head_ref,
     a0_ref,
@@ -292,34 +295,37 @@
             grad[it, owner, h] = gather_terms(way, h, k, owner)
             rs_copy(it, way, h, k, owner).start()
 
-        local(far)
-        send_raw(8, 0)
-        local_both(7)
-        send_raw(7, 0)
-        local_both(6)
-        local_both(5)
-        send_raw(5, 0)
+        targets = STOPS + [0]
+        early = LEAVES[targets[0]] + LEAVES[targets[1]]
+        for k in early:
+            if k == half_n:
+                local(far)
+            else:
+                local_both(k)
+            send_raw(k, 0)
+        local_both(targets[0])
         proj_t = proj[...].T
         resid = res_ref[...].astype(jnp.float32) + mm(mixed_t[...], proj_t, NN, HIGH)
         inner = mm(proj_t, resid * weighted, NT, HIGH)
-        send_raw(8, 1)
-        send_raw(7, 1)
-        send_raw(5, 1)
+        for k in early:
+            send_raw(k, 1)
         inner_start(it, 0, jnp.concatenate([inner[:half], inner[half:]], axis=1))
-        for k in (6, 4, 2):
+        for i, k in enumerate(STOPS):
+            later = LEAVES[targets[i + 2]] if i + 2 < len(targets) else []
             for way in range(2):
                 send_on(way, 0, k)
-            if k > 2:
-                local_both(k - 2)
-                local_both(k - 3)
-                send_raw(k - 3, 0)
+            if targets[i + 1]:
+                local_both(targets[i + 1])
             else:
                 local(z)
+            for leaf in later:
+                local_both(leaf)
+                send_raw(leaf, 0)
             for way in range(2):
                 send_on(way, 1, k)
-            if k > 2:
-                send_raw(k - 3, 1)
-            if k == 4:
+            for leaf in later:
+                send_raw(leaf, 1)
+            if i == len(STOPS) - 2:
                 inner_start(it, 1, inner_finish(it, 0))
         for h in range(2):
             total = grad[it, z, h]
@@ -333,7 +339,7 @@
             def _():
                 a_all[it, z, h] = own[h]
                 for way in range(2):
-                    ag_copy(it, way, h, 2, z).start()
+                    ag_copy(it, way, h, STOPS[-1], z).start()
 
         def inner_total():
             tile = inner_finish(it, 1)
@@ -363,54 +369,49 @@
                     if reaches(way, h, k):
                         ag_copy(it, way, h, k, toward(1 - way, parent)).start()
 
-            pass_on(0, 1, 0)
+            def pass_leaves(parent, h):
+                for k in LEAVES[parent]:
+                    pass_on(parent, k, h)
+
+            def use_leaves(parent):
+                for k in LEAVES[parent]:
+                    arrive(k, 0)
+                    arrive(k, 1)
+                    if k == half_n:
+                        proj[...] += project(far)
+                    else:
+                        use(k)
+
+            pass_leaves(0, 0)
             proj[...] = project(z)
-            pass_on(0, 1, 1)
-
-            arrive(2, 0)
-            pass_on(2, 4, 0)
-            step_inner = inner_total()
-            inner_sum[...] += step_inner
-            pass_on(2, 3, 0)
-            arrive(2, 1)
-            pass_on(2, 4, 1)
-            use(2)
-            pass_on(2, 3, 1)
-            arrive(1, 0)
-            arrive(1, 1)
-            use(1)
-
-            arrive(4, 0)
-            pass_on(4, 6, 0)
-            mixed[...] = mixed[...] - learn_rate * mm(step_inner, gram[...], NN, HIGH)
-            mixed_t[...] = mixed_t[...] - learn_rate * mm(gram[...], step_inner, NT, HIGH)
-            pass_on(4, 5, 0)
-            arrive(4, 1)
-            pass_on(4, 6, 1)
-            use(4)
-            pass_on(4, 5, 1)
-            arrive(3, 0)
-            arrive(3, 1)
-            use(3)
-
-            arrive(6, 0)
-            pass_on(6, 8, 0)
-            pass_on(6, 7, 0)
-            from_mixed()
-            arrive(6, 1)
-            pass_on(6, 8, 1)
-            pass_on(6, 7, 1)
-            use(6)
-            arrive(5, 0)
-            arrive(5, 1)
-            use(5)
-
-            arrive(7, 0)
-            arrive(7, 1)
-            use(7)
-            arrive(8, 0)
-            arrive(8, 1)
-            proj[...] += project(far)
+            pass_leaves(0, 1)
+            before = 0
+            for k in reversed(STOPS):
+                after = [c for c in CHILDREN[k] if CHILDREN[c]]
+                arrive(k, 0)
+                for c in after:
+                    pass_on(k, c, 0)
+                if before == 0:
+                    step_inner = inner_total()
+                    inner_sum[...] += step_inner
+                    mixed[...] = mixed[...] - learn_rate * mm(step_inner, gram[...], NN, HIGH)
+                if not after:
+                    pass_leaves(k, 0)
+                    mixed_t[...] = mixed_t[...] - learn_rate * mm(gram[...], step_inner, NT, HIGH)
+                    from_mixed()
+                else:
+                    pass_leaves(k, 0)
+                arrive(k, 1)
+                for c in after:
+                    pass_on(k, c, 1)
+                if not after:
+                    pass_leaves(k, 1)
+                use(k)
+                if after:
+                    pass_leaves(k, 1)
+                use_leaves(before)
+                before = k
+            use_leaves(before)
 
         return 0
 
@@ -513,20 +514,9 @@
     for k in range(1, chips):
         rd_copy(k).wait()
     for r in range(rank):
-        out_ref[r : r + 1, :] = row_done[r]
-
-
-def split(rows_ref, oin_ref, oout_ref, sem):
-    width_in = oin_ref.shape[1]
-    width_out = oout_ref.shape[1]
-    parts = (
-        pltpu.make_async_copy(rows_ref.at[:, pl.ds(0, width_in)], oin_ref, sem.at[0]),
-        pltpu.make_async_copy(rows_ref.at[:, pl.ds(width_in, width_out)], oout_ref, sem.at[1]),
-    )
-    for part in parts:
-        part.start()
-    for part in parts:
-        part.wait()
+        row = row_done[r]
+        oin_ref[r : r + 1, :] = row[:, :width_in]
+        oout_ref[r : r + 1, :] = row[:, width_in:]
 
 
 def on_device(
@@ -557,13 +547,16 @@
     hbm = pl.BlockSpec(memory_space=pltpu.HBM)
     vmem = pl.BlockSpec(memory_space=pltpu.VMEM)
     smem = pl.BlockSpec(memory_space=pltpu.SMEM)
-    rows = pl.pallas_call(
+    return pl.pallas_call(
         functools.partial(kernel, n, clients, out_scale),
-        out_shape=jax.ShapeDtypeStruct((rank, width), f32),
+        out_shape=(
+            jax.ShapeDtypeStruct((rank, width_in), f32),
+            jax.ShapeDtypeStruct((rank, width_out), f32),
+        ),
         in_specs=[
             hbm, hbm, hbm, hbm, hbm, smem, smem, hbm, hbm
         ],
-        out_specs=vmem,
+        out_specs=(vmem, vmem),
         scratch_shapes=[
             pltpu.VMEM((nout, tokens), jnp.bfloat16),
             pltpu.VMEM((nout, model_width), jnp.bfloat16),
@@ -621,17 +614,6 @@
         input_privacy_noise,
         output_privacy_noise,
     )
-    return pl.pallas_call(
-        split,
-        out_shape=(
-            jax.ShapeDtypeStruct((rank, width_in), f32),
-            jax.ShapeDtypeStruct((rank, width_out), f32),
-        ),
-        in_specs=[hbm],
-        out_specs=(hbm, hbm),
-        scratch_shapes=[dma((2,))],
-        compiler_params=pltpu.CompilerParams(vmem_limit_bytes=VMEM_BYTES),
-    )(rows)
 
 
 def solution(mesh):

time: 144 us -> 149 us (1.035)
  local copies, waits for them, and re-layouts: 0 us -> 2.77 us
  Pallas kernels: 142 us -> 144 us
    pallas_call x1, Pallas kernels: 139 us -> 144 us  [on_device(): pl.pallas_call(functools.partial(kernel, n, clients, out_scale), out_shap...]
    pallas_call x1 -> x0, Pallas kernels: 3.35 us -> none  [on_device(): pl.pallas_call(split, out_shape=(jax.ShapeDtypeStruct((rank, width_in), f...]
    unnamed x0 -> x2, local copies, waits for them, and re-layouts: none -> 2.77 us
where the time goes in v5:
time: 149 us
  Pallas kernels  144 us (97%)
  local copies, waits for them, and re-layouts  2.77 us (2%)
  between operations  1.93 us (1%)
    pallas_call x1, Pallas kernels, on_device(): pl.pallas_call(functools.partial(kernel, n, clients, out_scale), out_shap...  144 us

profile of v5, /device:TPU:1, one launch (start us, length us, event | category | flops | bytes accessed | tf_op | source)
XLA Modules:
  0.0 148.8 jit_solution(13948154789119562064)
XLA Ops:
  1.9 144.1 %shard_map.104 = (f32[16,896]{1,0:T(8,128)}, f32[16,256]{1,0:T(8,128)}) custom-call(bf16[1,128,14336]{2,1,0:T(8,128)(2,1)} %hid_ref.1, bf16[64,128]{1,0:T(8,128)(2,1)} %bitcast.5, bf16[64,4096]{1,0:T(8,128)(2,1)} %bitcast.4, bf16[16,14336]{1,0:T(8,128)(2,1)} %a0_hbm.1, bf16[16,4096]{1,0:T(8,128)(2,1)} %b0_hbm.1, s32[1,1]{1,0:T(1,128)S(6)} %copy.13.cnt_ref, ...), custom_call_target="tpu_custom_call" | custom-call | tf_op jit(solution)/shard_map/pallas_call | solution.py:550
  146.0 1.4 copy.15
  147.4 1.3 copy.16

commit v6 on v5

--- a/solution.py
+++ b/solution.py
@@ -17,7 +17,7 @@
 clip_bound = 0.001
 noise_mult = 0.1
 
-PARENT = {8: 6, 7: 6, 6: 3, 5: 3, 4: 3, 3: 0, 2: 0, 1: 0}
+PARENT = {8: 6, 7: 6, 6: 4, 5: 4, 4: 2, 3: 2, 2: 0, 1: 0}
 CHILDREN = {p: [k for k in PARENT if PARENT[k] == p] for p in range(9)}
 LEAVES = {p: [k for k in CHILDREN[p] if not CHILDREN[k]] for p in CHILDREN}
 STOPS = [k for k in PARENT if CHILDREN[k]]
@@ -73,6 +73,9 @@
     own,
     inner_out,
     inner_in,
+    count_out,
+    count_in,
+    count_far,
     spread,
     row_out,
     row_in,
@@ -85,6 +88,10 @@
     ag_recv,
     in_send,
     in_recv,
+    ct_send,
+    ct_recv,
+    cf_send,
+    cf_recv,
     sc_send,
     sc_recv,
     ro_send,
@@ -93,6 +100,7 @@
     rd_recv,
 ):
     half_n = n // 2
+    reach = n // 4
     chips = clients // CORES
     rank, width_in = nin_ref.shape
     width_out = nout_ref.shape[1]
@@ -112,6 +120,14 @@
 
     def at_chip(k):
         return lax.rem(chip + k, chips)
+
+    barrier = pltpu.get_barrier_semaphore()
+    for k in (reach, n - reach, *range(1, reach), *range(n - reach + 1, n)):
+        pl.semaphore_signal(barrier, inc=1, device_id={"dp": at_z(k)}, device_id_type=MESH)
+    for k in range(1, clients):
+        pl.semaphore_signal(
+            barrier, inc=1, device_id={"client": lax.rem(client + k, clients)}, device_id_type=MESH
+        )
 
     def load(j):
         return pltpu.make_async_copy(
@@ -138,14 +154,6 @@
     for piece in pieces[4:]:
         piece.start()
 
-    barrier = pltpu.get_barrier_semaphore()
-    for k in range(1, n):
-        pl.semaphore_signal(barrier, inc=1, device_id={"dp": at_z(k)}, device_id_type=MESH)
-    for k in range(1, clients):
-        pl.semaphore_signal(
-            barrier, inc=1, device_id={"client": lax.rem(client + k, clients)}, device_id_type=MESH
-        )
-
     for piece in pieces[:3]:
         piece.wait()
     head = head_ref[...]
@@ -163,32 +171,33 @@
     lane = lax.broadcasted_iota(jnp.int32, (1, tokens), 1)
     live = cnt_ref[0, 0]
 
-    pl.semaphore_wait(barrier, (n - 1) + (clients - 1))
-
-    def z_copy(which, k):
-        return pltpu.make_async_remote_copy(
-            src_ref=spread.at[which, z],
-            dst_ref=spread.at[which, z],
-            send_sem=sc_send.at[which, k],
-            recv_sem=sc_recv.at[which, k],
+    pl.semaphore_wait(barrier, 2 * reach + (clients - 1))
+
+    near = (*range(1, reach + 1), *range(n - reach, n))
+
+    def count_copy(k):
+        return pltpu.make_async_remote_copy(
+            src_ref=count_out.at[0],
+            dst_ref=count_in.at[n - k],
+            send_sem=ct_send.at[k],
+            recv_sem=ct_recv.at[n - k],
             device_id={"dp": at_z(k)},
             device_id_type=MESH,
         )
 
-    def z_start(which, row):
-        spread[which, z] = row
-        for k in range(1, n):
-            z_copy(which, k).start()
-
-    def z_finish(which):
-        for k in range(1, n):
-            z_copy(which, k).wait()
-        total = spread[which, 0]
-        for j in range(1, n):
-            total = total + spread[which, j]
-        return total
-
-    z_start(0, jnp.full((1, 128), live.astype(jnp.float32), jnp.float32))
+    def far_copy(way):
+        return pltpu.make_async_remote_copy(
+            src_ref=count_out.at[1 + way],
+            dst_ref=count_far.at[way],
+            send_sem=cf_send.at[way],
+            recv_sem=cf_recv.at[way],
+            device_id={"dp": at_z(n - reach) if way == 0 else at_z(reach)},
+            device_id_type=MESH,
+        )
+
+    count_out[0] = jnp.full((1, 128), live.astype(jnp.float32), jnp.float32)
+    for k in reversed(near):
+        count_copy(k).start()
 
     pieces[3].wait()
     proj[...] = jnp.zeros_like(proj)
@@ -206,7 +215,23 @@
     for h in range(2):
         own[h] = own_zero[h * half : (h + 1) * half]
     mask[...] = (lane < live).astype(jnp.float32)
-    tokens_live[...] = z_finish(0)
+
+    for k in near:
+        count_copy(n - k).wait_recv()
+    above = count_in[1]
+    for k in range(2, reach + 1):
+        above = above + count_in[k]
+    below = count_in[n - 1]
+    for k in range(2, reach):
+        below = below + count_in[n - k]
+    count_out[1] = above
+    count_out[2] = below
+    for way in range(2):
+        far_copy(way).start()
+    nearer = count_out[0] + above + below + count_in[n - reach]
+    for way in range(2):
+        far_copy(way).wait_recv()
+    tokens_live[...] = nearer + count_far[0] + count_far[1]
 
     def toward(way, k):
         return at_z(n - k) if way == 0 else at_z(k)
@@ -296,35 +321,31 @@
             rs_copy(it, way, h, k, owner).start()
 
         targets = STOPS + [0]
-        early = LEAVES[targets[0]] + LEAVES[targets[1]]
-        for k in early:
-            if k == half_n:
-                local(far)
-            else:
-                local_both(k)
-            send_raw(k, 0)
+
+        def send_leaves(i):
+            for k in LEAVES[targets[i]]:
+                if k == half_n:
+                    local(far)
+                else:
+                    local_both(k)
+                for h in range(2):
+                    send_raw(k, h)
+
+        send_leaves(0)
         local_both(targets[0])
+        send_leaves(1)
         proj_t = proj[...].T
         resid = res_ref[...].astype(jnp.float32) + mm(mixed_t[...], proj_t, NN, HIGH)
         inner = mm(proj_t, resid * weighted, NT, HIGH)
-        for k in early:
-            send_raw(k, 1)
         inner_start(it, 0, jnp.concatenate([inner[:half], inner[half:]], axis=1))
         for i, k in enumerate(STOPS):
-            later = LEAVES[targets[i + 2]] if i + 2 < len(targets) else []
-            for way in range(2):
-                send_on(way, 0, k)
+            for way, h in chains:
+                send_on(way, h, k)
             if targets[i + 1]:
                 local_both(targets[i + 1])
+                send_leaves(i + 2)
             else:
                 local(z)
-            for leaf in later:
-                local_both(leaf)
-                send_raw(leaf, 0)
-            for way in range(2):
-                send_on(way, 1, k)
-            for leaf in later:
-                send_raw(leaf, 1)
             if i == len(STOPS) - 2:
                 inner_start(it, 1, inner_finish(it, 0))
         for h in range(2):
@@ -359,56 +380,49 @@
                 for way in range(2):
                     proj[...] += project(toward(1 - way, k))
 
-            def arrive(k, h):
-                for way in range(2):
-                    if reaches(way, h, k):
-                        ag_copy(it, way, h, k, toward(1 - way, k)).wait_recv()
-
-            def pass_on(parent, k, h):
-                for way in range(2):
-                    if reaches(way, h, k):
-                        ag_copy(it, way, h, k, toward(1 - way, parent)).start()
-
-            def pass_leaves(parent, h):
+            def arrive(way, h, k):
+                if reaches(way, h, k):
+                    ag_copy(it, way, h, k, toward(1 - way, k)).wait_recv()
+
+            def pass_on(way, h, parent, k):
+                if reaches(way, h, k):
+                    ag_copy(it, way, h, k, toward(1 - way, parent)).start()
+
+            def pass_leaves(parent):
                 for k in LEAVES[parent]:
-                    pass_on(parent, k, h)
+                    for way, h in chains:
+                        pass_on(way, h, parent, k)
 
             def use_leaves(parent):
                 for k in LEAVES[parent]:
-                    arrive(k, 0)
-                    arrive(k, 1)
+                    for way, h in chains:
+                        arrive(way, h, k)
                     if k == half_n:
                         proj[...] += project(far)
                     else:
                         use(k)
 
-            pass_leaves(0, 0)
+            pass_leaves(0)
             proj[...] = project(z)
-            pass_leaves(0, 1)
+            step_inner = inner_total()
+            inner_sum[...] += step_inner
+            mixed[...] = mixed[...] - learn_rate * mm(step_inner, gram[...], NN, HIGH)
+            mixed_t[...] = mixed_t[...] - learn_rate * mm(gram[...], step_inner, NT, HIGH)
+            from_mixed()
             before = 0
             for k in reversed(STOPS):
-                after = [c for c in CHILDREN[k] if CHILDREN[c]]
-                arrive(k, 0)
-                for c in after:
-                    pass_on(k, c, 0)
-                if before == 0:
-                    step_inner = inner_total()
-                    inner_sum[...] += step_inner
-                    mixed[...] = mixed[...] - learn_rate * mm(step_inner, gram[...], NN, HIGH)
-                if not after:
-                    pass_leaves(k, 0)
-                    mixed_t[...] = mixed_t[...] - learn_rate * mm(gram[...], step_inner, NT, HIGH)
-                    from_mixed()
+                for way, h in chains:
+                    arrive(way, h, k)
+                    for c in CHILDREN[k]:
+                        if CHILDREN[c]:
+                            pass_on(way, h, k, c)
+                if k < STOPS[0]:
+                    proj[...] += project(toward(1, k))
+                pass_leaves(k)
+                if k < STOPS[0]:
+                    proj[...] += project(toward(0, k))
                 else:
-                    pass_leaves(k, 0)
-                arrive(k, 1)
-                for c in after:
-                    pass_on(k, c, 1)
-                if not after:
-                    pass_leaves(k, 1)
-                use(k)
-                if after:
-                    pass_leaves(k, 1)
+                    use(k)
                 use_leaves(before)
                 before = k
             use_leaves(before)
@@ -416,6 +430,29 @@
         return 0
 
     lax.fori_loop(0, ITERS, local_step, 0)
+
+    def z_copy(k):
+        return pltpu.make_async_remote_copy(
+            src_ref=spread.at[z],
+            dst_ref=spread.at[z],
+            send_sem=sc_send.at[k],
+            recv_sem=sc_recv.at[k],
+            device_id={"dp": at_z(k)},
+            device_id_type=MESH,
+        )
+
+    def z_start(row):
+        spread[z] = row
+        for k in sorted(range(1, n), key=lambda k: -min(k, n - k)):
+            z_copy(k).start()
+
+    def z_finish():
+        for k in range(1, n):
+            z_copy(k).wait()
+        total = spread[0]
+        for j in range(1, n):
+            total = total + spread[j]
+        return total
 
     own_three = jnp.concatenate([own[0], own[1]], axis=0)
     delta_in = own_three - own_zero
@@ -460,7 +497,7 @@
     for c in range(1, clients):
         ends = ends + row_in[c][:, width:]
 
-    z_start(1, ends[:, :128])
+    z_start(ends[:, :128])
     for piece in pieces[4:]:
         piece.wait()
     noise = jnp.concatenate(
@@ -468,7 +505,7 @@
     )
     weights = ends[:, 128:]
     wsum = jnp.sum(weights, axis=1, keepdims=True)
-    scales = weights * jnp.minimum(1.0, clip_bound / jnp.sqrt(z_finish(1) + 1e-06))
+    scales = weights * jnp.minimum(1.0, clip_bound / jnp.sqrt(z_finish() + 1e-06))
     row = scales[:, :1] * row_in[0][:, :width]
     for c in range(1, clients):
         row = row + scales[:, c : c + 1] * row_in[c][:, :width]
@@ -506,6 +543,10 @@
         return 0
 
     lax.fori_loop(0, ITERS, drain_step, 0)
+    for k in near:
+        count_copy(k).wait_send()
+    for way in range(2):
+        far_copy(way).wait_send()
 
     for k in range(1, chips):
         for to_core in range(CORES):
@@ -581,7 +622,10 @@
             pltpu.VMEM((2, half, width_in), f32),
             pltpu.VMEM((ITERS, 2, half, 128), f32),
             pltpu.VMEM((ITERS, 2, BLOCK - 1, half, 128), f32),
-            pltpu.VMEM((2, n, 1, 128), f32),
+            pltpu.VMEM((3, 1, 128), f32),
+            pltpu.VMEM((n, 1, 128), f32),
+            pltpu.VMEM((2, 1, 128), f32),
+            pltpu.VMEM((n, 1, 128), f32),
             pltpu.VMEM((rank, 1, width + 256), f32),
             pltpu.VMEM((clients, 1, width + 256), f32),
             pltpu.VMEM((rank, 1, width), f32),
@@ -593,8 +637,12 @@
             dma((ITERS - 1, 2, 2, half_n)),
             dma((ITERS, 2, BLOCK - 1)),
             dma((ITERS, 2, BLOCK - 1)),
-            dma((2, n)),
-            dma((2, n)),
+            dma((n,)),
+            dma((n,)),
+            dma((2,)),
+            dma((2,)),
+            dma((n,)),
+            dma((n,)),
             dma((chips, CORES)),
             dma((chips, CORES)),
             dma((chips,)),

time: 149 us -> 147 us (0.987)
  Pallas kernels: 144 us -> 142 us
    pallas_call x1, Pallas kernels: 144 us -> 142 us  [on_device(): pl.pallas_call(functools.partial(kernel, n, clients, out_scale), out_shap...]
where the time goes in v6:
time: 147 us; the launch traced here: 146 us
  Pallas kernels  142 us (97%)
  local copies, waits for them, and re-layouts  2.77 us (2%)
  between operations  1.93 us (1%)
    pallas_call x1, Pallas kernels, on_device(): pl.pallas_call(functools.partial(kernel, n, clients, out_scale), out_shap...  142 us

profile of v6, /device:TPU:1, one launch (start us, length us, event | category | flops | bytes accessed | tf_op | source)
XLA Modules:
  0.0 146.5 jit_solution(13874606415731789471)
XLA Ops:
  1.9 141.8 %shard_map.104 = (f32[16,896]{1,0:T(8,128)}, f32[16,256]{1,0:T(8,128)}) custom-call(bf16[1,128,14336]{2,1,0:T(8,128)(2,1)} %hid_ref.1, bf16[64,128]{1,0:T(8,128)(2,1)} %bitcast.5, bf16[64,4096]{1,0:T(8,128)(2,1)} %bitcast.4, bf16[16,14336]{1,0:T(8,128)(2,1)} %a0_hbm.1, bf16[16,4096]{1,0:T(8,128)(2,1)} %b0_hbm.1, s32[1,1]{1,0:T(1,128)S(6)} %copy.13.cnt_ref, ...), custom_call_target="tpu_custom_call" | custom-call | tf_op jit(solution)/shard_map/pallas_call | solution.py:591
  143.7 1.4 copy.15
  145.2 1.3 copy.16

commit v7 on v5

--- a/solution.py
+++ b/solution.py
@@ -17,7 +17,7 @@
 clip_bound = 0.001
 noise_mult = 0.1
 
-PARENT = {8: 6, 7: 6, 6: 3, 5: 3, 4: 3, 3: 0, 2: 0, 1: 0}
+PARENT = {8: 6, 7: 6, 6: 4, 5: 4, 4: 2, 3: 2, 2: 0, 1: 0}
 CHILDREN = {p: [k for k in PARENT if PARENT[k] == p] for p in range(9)}
 LEAVES = {p: [k for k in CHILDREN[p] if not CHILDREN[k]] for p in CHILDREN}
 STOPS = [k for k in PARENT if CHILDREN[k]]
@@ -295,37 +295,44 @@
             grad[it, owner, h] = gather_terms(way, h, k, owner)
             rs_copy(it, way, h, k, owner).start()
 
-        targets = STOPS + [0]
-        early = LEAVES[targets[0]] + LEAVES[targets[1]]
-        for k in early:
-            if k == half_n:
-                local(far)
-            else:
-                local_both(k)
-            send_raw(k, 0)
-        local_both(targets[0])
+        def left(h, *places):
+            for k in places:
+                for way in range(2):
+                    if reaches(way, h, k):
+                        rs_copy(it, way, h, k, z).wait_send()
+
+        local(far)
+        send_raw(8, 0)
+        local_both(7)
+        send_raw(7, 0)
+        local_both(6)
+        left(0, 8, 7)
+        send_raw(8, 1)
+        send_raw(7, 1)
+        local_both(5)
         proj_t = proj[...].T
         resid = res_ref[...].astype(jnp.float32) + mm(mixed_t[...], proj_t, NN, HIGH)
         inner = mm(proj_t, resid * weighted, NT, HIGH)
-        for k in early:
-            send_raw(k, 1)
+        left(1, 8, 7)
+        send_raw(5, 0)
+        send_raw(5, 1)
         inner_start(it, 0, jnp.concatenate([inner[:half], inner[half:]], axis=1))
-        for i, k in enumerate(STOPS):
-            later = LEAVES[targets[i + 2]] if i + 2 < len(targets) else []
+        for k in STOPS:
             for way in range(2):
                 send_on(way, 0, k)
-            if targets[i + 1]:
-                local_both(targets[i + 1])
+            if k > 2:
+                local_both(k - 2)
             else:
                 local(z)
-            for leaf in later:
-                local_both(leaf)
-                send_raw(leaf, 0)
+            left(0, k)
             for way in range(2):
                 send_on(way, 1, k)
-            for leaf in later:
-                send_raw(leaf, 1)
-            if i == len(STOPS) - 2:
+            if k > 2:
+                local_both(k - 3)
+                left(1, k)
+                for h in range(2):
+                    send_raw(k - 3, h)
+            if k == 4:
                 inner_start(it, 1, inner_finish(it, 0))
         for h in range(2):
             total = grad[it, z, h]
@@ -382,36 +389,43 @@
                     else:
                         use(k)
 
+            def gone(h, k):
+                for way in range(2):
+                    ag_copy(it, way, h, k, z).wait_send()
+
+            proj[...] = project(z)
+            step_inner = inner_total()
+            inner_sum[...] += step_inner
+            gone(0, STOPS[-1])
+            gone(1, STOPS[-1])
             pass_leaves(0, 0)
-            proj[...] = project(z)
             pass_leaves(0, 1)
-            before = 0
+            mixed[...] = mixed[...] - learn_rate * mm(step_inner, gram[...], NN, HIGH)
+            mixed_t[...] = mixed_t[...] - learn_rate * mm(gram[...], step_inner, NT, HIGH)
+            passed = [0]
             for k in reversed(STOPS):
-                after = [c for c in CHILDREN[k] if CHILDREN[c]]
+                onward = [c for c in CHILDREN[k] if CHILDREN[c]]
                 arrive(k, 0)
-                for c in after:
+                for c in onward or LEAVES[k]:
                     pass_on(k, c, 0)
-                if before == 0:
-                    step_inner = inner_total()
-                    inner_sum[...] += step_inner
-                    mixed[...] = mixed[...] - learn_rate * mm(step_inner, gram[...], NN, HIGH)
-                if not after:
-                    pass_leaves(k, 0)
-                    mixed_t[...] = mixed_t[...] - learn_rate * mm(gram[...], step_inner, NT, HIGH)
+                if k == STOPS[-1]:
                     from_mixed()
                 else:
+                    use_leaves(passed[-2])
+                for c in onward:
+                    gone(0, c)
+                arrive(k, 1)
+                for c in onward or LEAVES[k]:
+                    pass_on(k, c, 1)
+                use(k)
+                if onward:
+                    for c in onward:
+                        gone(1, c)
                     pass_leaves(k, 0)
-                arrive(k, 1)
-                for c in after:
-                    pass_on(k, c, 1)
-                if not after:
                     pass_leaves(k, 1)
-                use(k)
-                if after:
-                    pass_leaves(k, 1)
-                use_leaves(before)
-                before = k
-            use_leaves(before)
+                passed.append(k)
+            use_leaves(passed[-2])
+            use_leaves(passed[-1])
 
         return 0
 
@@ -489,9 +503,10 @@
 
     def drain_step(it, _):
         for way, h in chains:
-            for k in PARENT:
-                if reaches(way, h, k):
-                    rs_copy(it, way, h, k, z).wait_send()
+            for k in (5, 3, 1):
+                rs_copy(it, way, h, k, z).wait_send()
+            if h == 1:
+                rs_copy(it, way, h, STOPS[-1], z).wait_send()
         for stage in range(2):
             for j in range(1, BLOCK):
                 inner_copy(it, stage, j).wait_send()
@@ -499,7 +514,7 @@
         @pl.when(it < ITERS - 1)
         def _():
             for way, h in chains:
-                for k in PARENT:
+                for k in (8, 7, 5, 3, 1):
                     if reaches(way, h, k):
                         ag_copy(it, way, h, k, z).wait_send()
 

time: 149 us -> 154 us (1.034)
  Pallas kernels: 144 us -> 149 us
    pallas_call x1, Pallas kernels: 144 us -> 149 us  [on_device(): pl.pallas_call(functools.partial(kernel, n, clients, out_scale), out_shap...]
where the time goes in v7:
time: 154 us; the launch traced here: 153 us
  Pallas kernels  149 us (97%)
  local copies, waits for them, and re-layouts  2.77 us (2%)
  between operations  1.93 us (1%)
    pallas_call x1, Pallas kernels, on_device(): pl.pallas_call(functools.partial(kernel, n, clients, out_scale), out_shap...  149 us

profile of v7, /device:TPU:1, one launch (start us, length us, event | category | flops | bytes accessed | tf_op | source)
XLA Modules:
  0.0 153.4 jit_solution(14665902795735742776)
XLA Ops:
  1.9 148.7 %shard_map.104 = (f32[16,896]{1,0:T(8,128)}, f32[16,256]{1,0:T(8,128)}) custom-call(bf16[1,128,14336]{2,1,0:T(8,128)(2,1)} %hid_ref.1, bf16[64,128]{1,0:T(8,128)(2,1)} %bitcast.5, bf16[64,4096]{1,0:T(8,128)(2,1)} %bitcast.4, bf16[16,14336]{1,0:T(8,128)(2,1)} %a0_hbm.1, bf16[16,4096]{1,0:T(8,128)(2,1)} %b0_hbm.1, s32[1,1]{1,0:T(1,128)S(6)} %copy.13.cnt_ref, ...), custom_call_target="tpu_custom_call" | custom-call | tf_op jit(solution)/shard_map/pallas_call | solution.py:565
  150.7 1.4 copy.15
  152.1 1.3 copy.16

commit v8 on v5

--- a/solution.py
+++ b/solution.py
@@ -17,10 +17,9 @@
 clip_bound = 0.001
 noise_mult = 0.1
 
-PARENT = {8: 6, 7: 6, 6: 3, 5: 3, 4: 3, 3: 0, 2: 0, 1: 0}
+PARENT = {8: 7, 7: 6, 6: 5, 5: 4, 4: 2, 3: 2, 2: 0, 1: 0}
 CHILDREN = {p: [k for k in PARENT if PARENT[k] == p] for p in range(9)}
-LEAVES = {p: [k for k in CHILDREN[p] if not CHILDREN[k]] for p in CHILDREN}
-STOPS = [k for k in PARENT if CHILDREN[k]]
+CHAIN = (8, 7, 6, 5, 4, 2)
 
 MESH = pl.DeviceIdType.MESH
 HIGH = lax.Precision.HIGHEST
@@ -295,38 +294,43 @@
             grad[it, owner, h] = gather_terms(way, h, k, owner)
             rs_copy(it, way, h, k, owner).start()
 
-        targets = STOPS + [0]
-        early = LEAVES[targets[0]] + LEAVES[targets[1]]
-        for k in early:
-            if k == half_n:
-                local(far)
-            else:
-                local_both(k)
-            send_raw(k, 0)
-        local_both(targets[0])
+        def step(h, i):
+            send_on(h, h, CHAIN[i])
+            if i + 1 < len(CHAIN):
+                send_on(1 - h, h, CHAIN[i + 1])
+
+        local(far)
+        send_raw(8, 0)
+        local_both(7)
+        rs_copy(it, 1, 0, 7, toward(1, 7)).start()
+        local_both(6)
         proj_t = proj[...].T
         resid = res_ref[...].astype(jnp.float32) + mm(mixed_t[...], proj_t, NN, HIGH)
         inner = mm(proj_t, resid * weighted, NT, HIGH)
-        for k in early:
-            send_raw(k, 1)
+        send_raw(8, 1)
+        rs_copy(it, 0, 1, 7, toward(0, 7)).start()
         inner_start(it, 0, jnp.concatenate([inner[:half], inner[half:]], axis=1))
-        for i, k in enumerate(STOPS):
-            later = LEAVES[targets[i + 2]] if i + 2 < len(targets) else []
-            for way in range(2):
-                send_on(way, 0, k)
-            if targets[i + 1]:
-                local_both(targets[i + 1])
-            else:
-                local(z)
-            for leaf in later:
-                local_both(leaf)
-                send_raw(leaf, 0)
-            for way in range(2):
-                send_on(way, 1, k)
-            for leaf in later:
-                send_raw(leaf, 1)
-            if i == len(STOPS) - 2:
-                inner_start(it, 1, inner_finish(it, 0))
+        local_both(5)
+        step(0, 1)
+        local_both(4)
+        local_both(3)
+        send_raw(3, 0)
+        step(1, 1)
+        send_raw(3, 1)
+        step(0, 2)
+        local_both(2)
+        local_both(1)
+        send_raw(1, 0)
+        step(1, 2)
+        send_raw(1, 1)
+        step(0, 3)
+        local(z)
+        step(1, 3)
+        step(0, 4)
+        inner_start(it, 1, inner_finish(it, 0))
+        step(1, 4)
+        step(0, 5)
+        step(1, 5)
         for h in range(2):
             total = grad[it, z, h]
             for way in range(2):
@@ -339,7 +343,7 @@
             def _():
                 a_all[it, z, h] = own[h]
                 for way in range(2):
-                    ag_copy(it, way, h, STOPS[-1], z).start()
+                    ag_copy(it, way, h, CHAIN[-1], z).start()
 
         def inner_total():
             tile = inner_finish(it, 1)
@@ -359,59 +363,54 @@
                 for way in range(2):
                     proj[...] += project(toward(1 - way, k))
 
-            def arrive(k, h):
-                for way in range(2):
-                    if reaches(way, h, k):
-                        ag_copy(it, way, h, k, toward(1 - way, k)).wait_recv()
-
-            def pass_on(parent, k, h):
-                for way in range(2):
-                    if reaches(way, h, k):
-                        ag_copy(it, way, h, k, toward(1 - way, parent)).start()
-
-            def pass_leaves(parent, h):
-                for k in LEAVES[parent]:
-                    pass_on(parent, k, h)
-
-            def use_leaves(parent):
-                for k in LEAVES[parent]:
-                    arrive(k, 0)
-                    arrive(k, 1)
-                    if k == half_n:
-                        proj[...] += project(far)
-                    else:
-                        use(k)
-
-            pass_leaves(0, 0)
+            def arrive(way, h, k):
+                if reaches(way, h, k):
+                    ag_copy(it, way, h, k, toward(1 - way, k)).wait_recv()
+
+            def pass_on(way, h, parent, k):
+                if reaches(way, h, k):
+                    ag_copy(it, way, h, k, toward(1 - way, parent)).start()
+
+            def relay(h, k, onward):
+                for way in (h, 1 - h):
+                    arrive(way, h, k)
+                    pass_on(way, h, k, onward)
+
+            def use_leaf(k):
+                for way, h in chains:
+                    arrive(way, h, k)
+                use(k)
+
+            for way, h in chains:
+                pass_on(way, h, 0, 1)
             proj[...] = project(z)
-            pass_leaves(0, 1)
-            before = 0
-            for k in reversed(STOPS):
-                after = [c for c in CHILDREN[k] if CHILDREN[c]]
-                arrive(k, 0)
-                for c in after:
-                    pass_on(k, c, 0)
-                if before == 0:
-                    step_inner = inner_total()
-                    inner_sum[...] += step_inner
-                    mixed[...] = mixed[...] - learn_rate * mm(step_inner, gram[...], NN, HIGH)
-                if not after:
-                    pass_leaves(k, 0)
-                    mixed_t[...] = mixed_t[...] - learn_rate * mm(gram[...], step_inner, NT, HIGH)
-                    from_mixed()
-                else:
-                    pass_leaves(k, 0)
-                arrive(k, 1)
-                for c in after:
-                    pass_on(k, c, 1)
-                if not after:
-                    pass_leaves(k, 1)
-                use(k)
-                if after:
-                    pass_leaves(k, 1)
-                use_leaves(before)
-                before = k
-            use_leaves(before)
+            step_inner = inner_total()
+            inner_sum[...] += step_inner
+            mixed[...] = mixed[...] - learn_rate * mm(step_inner, gram[...], NN, HIGH)
+            relay(0, 2, 4)
+            mixed_t[...] = mixed_t[...] - learn_rate * mm(gram[...], step_inner, NT, HIGH)
+            relay(1, 2, 4)
+            for way, h in chains:
+                pass_on(way, h, 2, 3)
+            use(2)
+            from_mixed()
+            relay(0, 4, 5)
+            use_leaf(1)
+            relay(1, 4, 5)
+            use(4)
+            relay(0, 5, 6)
+            use_leaf(3)
+            relay(1, 5, 6)
+            use(5)
+            relay(0, 6, 7)
+            relay(1, 6, 7)
+            use(6)
+            relay(0, 7, 8)
+            relay(1, 7, 8)
+            use(7)
+            arrive(0, 0, 8)
+            arrive(1, 1, 8)
+            proj[...] += project(far)
 
         return 0
 

time: 149 us -> 162 us (1.087)
  Pallas kernels: 144 us -> 157 us
    pallas_call x1, Pallas kernels: 144 us -> 157 us  [on_device(): pl.pallas_call(functools.partial(kernel, n, clients, out_scale), out_shap...]
where the time goes in v8:
time: 162 us
  Pallas kernels  157 us (97%)
  local copies, waits for them, and re-layouts  2.77 us (2%)
  between operations  1.93 us (1%)
    pallas_call x1, Pallas kernels, on_device(): pl.pallas_call(functools.partial(kernel, n, clients, out_scale), out_shap...  157 us

profile of v8, /device:TPU:1, one launch (start us, length us, event | category | flops | bytes accessed | tf_op | source)
XLA Modules:
  0.0 161.8 jit_solution(2498768303102848496)
XLA Ops:
  1.9 157.1 %shard_map.104 = (f32[16,896]{1,0:T(8,128)}, f32[16,256]{1,0:T(8,128)}) custom-call(bf16[1,128,14336]{2,1,0:T(8,128)(2,1)} %hid_ref.1, bf16[64,128]{1,0:T(8,128)(2,1)} %bitcast.5, bf16[64,4096]{1,0:T(8,128)(2,1)} %bitcast.4, bf16[16,14336]{1,0:T(8,128)(2,1)} %a0_hbm.1, bf16[16,4096]{1,0:T(8,128)(2,1)} %b0_hbm.1, s32[1,1]{1,0:T(1,128)S(6)} %copy.13.cnt_ref, ...), custom_call_target="tpu_custom_call" | custom-call | tf_op jit(solution)/shard_map/pallas_call | solution.py:549
  159.0 1.4 copy.15
  160.4 1.3 copy.16

commit v9 on v5

--- a/solution.py
+++ b/solution.py
@@ -17,7 +17,7 @@
 clip_bound = 0.001
 noise_mult = 0.1
 
-PARENT = {8: 6, 7: 6, 6: 3, 5: 3, 4: 3, 3: 0, 2: 0, 1: 0}
+PARENT = {8: 6, 7: 6, 6: 4, 5: 4, 4: 2, 3: 2, 2: 0, 1: 0}
 CHILDREN = {p: [k for k in PARENT if PARENT[k] == p] for p in range(9)}
 LEAVES = {p: [k for k in CHILDREN[p] if not CHILDREN[k]] for p in CHILDREN}
 STOPS = [k for k in PARENT if CHILDREN[k]]
@@ -211,22 +211,25 @@
     def toward(way, k):
         return at_z(n - k) if way == 0 else at_z(k)
 
-    def rs_copy(it, way, h, k, owner):
+    def chunk(ref, way, k):
+        return ref.at[way] if k == half_n else ref
+
+    def rs_copy(it, way, k, owner):
         return pltpu.make_async_remote_copy(
-            src_ref=grad.at[it, owner, h],
-            dst_ref=slot.at[it, way, h, k - 1],
-            send_sem=rs_send.at[it, way, h, k - 1],
-            recv_sem=rs_recv.at[it, way, h, k - 1],
+            src_ref=chunk(grad.at[it, owner], way, k),
+            dst_ref=chunk(slot.at[it, way, k - 1], way, k),
+            send_sem=rs_send.at[it, way, k - 1],
+            recv_sem=rs_recv.at[it, way, k - 1],
             device_id={"dp": toward(way, k - PARENT[k])},
             device_id_type=MESH,
         )
 
-    def ag_copy(it, way, h, k, owner):
+    def ag_copy(it, way, k, owner):
         return pltpu.make_async_remote_copy(
-            src_ref=a_all.at[it, owner, h],
-            dst_ref=a_all.at[it, owner, h],
-            send_sem=ag_send.at[it, way, h, k - 1],
-            recv_sem=ag_recv.at[it, way, h, k - 1],
+            src_ref=chunk(a_all.at[it, owner], way, k),
+            dst_ref=chunk(a_all.at[it, owner], way, k),
+            send_sem=ag_send.at[it, way, k - 1],
+            recv_sem=ag_recv.at[it, way, k - 1],
             device_id={"dp": toward(way, k - PARENT[k])},
             device_id_type=MESH,
         )
@@ -254,13 +257,6 @@
             total = total + inner_in[it, stage, j - 1]
         return total
 
-    def long(way, h):
-        return way == h
-
-    def reaches(way, h, k):
-        return k < half_n or long(way, h)
-
-    chains = ((0, 0), (1, 1), (0, 1), (1, 0))
     far = at_z(half_n)
 
     def local_step(it, _):
@@ -277,69 +273,61 @@
             for way in range(2):
                 local(toward(way, k))
 
-        def send_raw(k, h):
-            for way in range(2):
-                if reaches(way, h, k):
-                    rs_copy(it, way, h, k, toward(way, k)).start()
-
-        def gather_terms(way, h, k, owner):
-            total = grad[it, owner, h]
+        def add_terms(way, k, owner, total):
             for child in reversed(CHILDREN[k]):
-                if reaches(way, h, child):
-                    rs_copy(it, way, h, child, owner).wait_recv()
-                    total = total + slot[it, way, h, child - 1]
+                rs_copy(it, way, child, owner).wait_recv()
+                for h in range(2):
+                    if child < half_n or h == way:
+                        total[h] = total[h] + slot[it, way, child - 1, h]
             return total
 
-        def send_on(way, h, k):
+        def send_on(way, k):
             owner = toward(way, k)
-            grad[it, owner, h] = gather_terms(way, h, k, owner)
-            rs_copy(it, way, h, k, owner).start()
+            total = add_terms(way, k, owner, [grad[it, owner, h] for h in range(2)])
+            for h in range(2):
+                grad[it, owner, h] = total[h]
+            rs_copy(it, way, k, owner).start()
 
         targets = STOPS + [0]
-        early = LEAVES[targets[0]] + LEAVES[targets[1]]
-        for k in early:
-            if k == half_n:
-                local(far)
-            else:
-                local_both(k)
-            send_raw(k, 0)
+
+        def send_leaves(i):
+            for k in LEAVES[targets[i]]:
+                if k == half_n:
+                    local(far)
+                else:
+                    local_both(k)
+                for way in range(2):
+                    rs_copy(it, way, k, toward(way, k)).start()
+
+        send_leaves(0)
         local_both(targets[0])
+        send_leaves(1)
         proj_t = proj[...].T
         resid = res_ref[...].astype(jnp.float32) + mm(mixed_t[...], proj_t, NN, HIGH)
         inner = mm(proj_t, resid * weighted, NT, HIGH)
-        for k in early:
-            send_raw(k, 1)
         inner_start(it, 0, jnp.concatenate([inner[:half], inner[half:]], axis=1))
         for i, k in enumerate(STOPS):
-            later = LEAVES[targets[i + 2]] if i + 2 < len(targets) else []
             for way in range(2):
-                send_on(way, 0, k)
+                send_on(way, k)
             if targets[i + 1]:
                 local_both(targets[i + 1])
+                send_leaves(i + 2)
             else:
                 local(z)
-            for leaf in later:
-                local_both(leaf)
-                send_raw(leaf, 0)
-            for way in range(2):
-                send_on(way, 1, k)
-            for leaf in later:
-                send_raw(leaf, 1)
             if i == len(STOPS) - 2:
                 inner_start(it, 1, inner_finish(it, 0))
+        total = [grad[it, z, h] for h in range(2)]
+        for way in range(2):
+            total = add_terms(way, 0, z, total)
         for h in range(2):
-            total = grad[it, z, h]
+            own[h] = own[h] - learn_rate * total[h]
+
+        @pl.when(it < ITERS - 1)
+        def _():
+            for h in range(2):
+                a_all[it, z, h] = own[h]
             for way in range(2):
-                for child in CHILDREN[0]:
-                    rs_copy(it, way, h, child, z).wait_recv()
-                    total = total + slot[it, way, h, child - 1]
-            own[h] = own[h] - learn_rate * total
-
-            @pl.when(it < ITERS - 1)
-            def _():
-                a_all[it, z, h] = own[h]
-                for way in range(2):
-                    ag_copy(it, way, h, STOPS[-1], z).start()
+                ag_copy(it, way, STOPS[-1], z).start()
 
         def inner_total():
             tile = inner_finish(it, 1)
@@ -359,56 +347,47 @@
                 for way in range(2):
                     proj[...] += project(toward(1 - way, k))
 
-            def arrive(k, h):
-                for way in range(2):
-                    if reaches(way, h, k):
-                        ag_copy(it, way, h, k, toward(1 - way, k)).wait_recv()
-
-            def pass_on(parent, k, h):
-                for way in range(2):
-                    if reaches(way, h, k):
-                        ag_copy(it, way, h, k, toward(1 - way, parent)).start()
-
-            def pass_leaves(parent, h):
+            def arrive(way, k):
+                ag_copy(it, way, k, toward(1 - way, k)).wait_recv()
+
+            def pass_on(way, parent, k):
+                ag_copy(it, way, k, toward(1 - way, parent)).start()
+
+            def pass_leaves(parent):
                 for k in LEAVES[parent]:
-                    pass_on(parent, k, h)
+                    for way in range(2):
+                        pass_on(way, parent, k)
 
             def use_leaves(parent):
                 for k in LEAVES[parent]:
-                    arrive(k, 0)
-                    arrive(k, 1)
+                    for way in range(2):
+                        arrive(way, k)
                     if k == half_n:
                         proj[...] += project(far)
                     else:
                         use(k)
 
-            pass_leaves(0, 0)
+            pass_leaves(0)
             proj[...] = project(z)
-            pass_leaves(0, 1)
+            step_inner = inner_total()
+            inner_sum[...] += step_inner
+            mixed[...] = mixed[...] - learn_rate * mm(step_inner, gram[...], NN, HIGH)
+            mixed_t[...] = mixed_t[...] - learn_rate * mm(gram[...], step_inner, NT, HIGH)
+            from_mixed()
             before = 0
             for k in reversed(STOPS):
-                after = [c for c in CHILDREN[k] if CHILDREN[c]]
-                arrive(k, 0)
-                for c in after:
-                    pass_on(k, c, 0)
-                if before == 0:
-                    step_inner = inner_total()
-                    inner_sum[...] += step_inner
-                    mixed[...] = mixed[...] - learn_rate * mm(step_inner, gram[...], NN, HIGH)
-                if not after:
-                    pass_leaves(k, 0)
-                    mixed_t[...] = mixed_t[...] - learn_rate * mm(gram[...], step_inner, NT, HIGH)
-                    from_mixed()
+                for way in range(2):
+                    arrive(way, k)
+                    for c in CHILDREN[k]:
+                        if CHILDREN[c]:
+                            pass_on(way, k, c)
+                if k < STOPS[0]:
+                    proj[...] += project(toward(1, k))
+                pass_leaves(k)
+                if k < STOPS[0]:
+                    proj[...] += project(toward(0, k))
                 else:
-                    pass_leaves(k, 0)
-                arrive(k, 1)
-                for c in after:
-                    pass_on(k, c, 1)
-                if not after:
-                    pass_leaves(k, 1)
-                use(k)
-                if after:
-                    pass_leaves(k, 1)
+                    use(k)
                 use_leaves(before)
                 before = k
             use_leaves(before)
@@ -488,20 +467,18 @@
         rd_copy(k).start()
 
     def drain_step(it, _):
-        for way, h in chains:
+        for way in range(2):
             for k in PARENT:
-                if reaches(way, h, k):
-                    rs_copy(it, way, h, k, z).wait_send()
+                rs_copy(it, way, k, z).wait_send()
         for stage in range(2):
             for j in range(1, BLOCK):
                 inner_copy(it, stage, j).wait_send()
 
         @pl.when(it < ITERS - 1)
         def _():
-            for way, h in chains:
+            for way in range(2):
                 for k in PARENT:
-                    if reaches(way, h, k):
-                        ag_copy(it, way, h, k, z).wait_send()
+                    ag_copy(it, way, k, z).wait_send()
 
         return 0
 
@@ -576,7 +553,7 @@
             pltpu.VMEM((rank, rank), f32),
             pltpu.VMEM((rank, tokens), f32),
             pltpu.VMEM((ITERS, n, 2, half, width_in), f32),
-            pltpu.VMEM((ITERS, 2, 2, half_n, half, width_in), f32),
+            pltpu.VMEM((ITERS, 2, half_n, 2, half, width_in), f32),
             pltpu.VMEM((ITERS - 1, n, 2, half, width_in), f32),
             pltpu.VMEM((2, half, width_in), f32),
             pltpu.VMEM((ITERS, 2, half, 128), f32),
@@ -587,10 +564,10 @@
             pltpu.VMEM((rank, 1, width), f32),
             dma((6,)),
             dma((n,)),
-            dma((ITERS, 2, 2, half_n)),
-            dma((ITERS, 2, 2, half_n)),
-            dma((ITERS - 1, 2, 2, half_n)),
-            dma((ITERS - 1, 2, 2, half_n)),
+            dma((ITERS, 2, half_n)),
+            dma((ITERS, 2, half_n)),
+            dma((ITERS - 1, 2, half_n)),
+            dma((ITERS - 1, 2, half_n)),
             dma((ITERS, 2, BLOCK - 1)),
             dma((ITERS, 2, BLOCK - 1)),
             dma((2, n)),

time: 149 us -> 149 us (level)
  no operation moved by 1% of the time
where the time goes in v9:
time: 149 us
  Pallas kernels  144 us (97%)
  local copies, waits for them, and re-layouts  2.77 us (2%)
  between operations  1.93 us (1%)
    pallas_call x1, Pallas kernels, on_device(): pl.pallas_call(functools.partial(kernel, n, clients, out_scale), out_shap...  144 us

profile of v9, /device:TPU:1, one launch (start us, length us, event | category | flops | bytes accessed | tf_op | source)
XLA Modules:
  0.0 148.7 jit_solution(16280261299145532464)
XLA Ops:
  1.9 144.0 %shard_map.104 = (f32[16,896]{1,0:T(8,128)}, f32[16,256]{1,0:T(8,128)}) custom-call(bf16[1,128,14336]{2,1,0:T(8,128)(2,1)} %hid_ref.1, bf16[64,128]{1,0:T(8,128)(2,1)} %bitcast.5, bf16[64,4096]{1,0:T(8,128)(2,1)} %bitcast.4, bf16[16,14336]{1,0:T(8,128)(2,1)} %a0_hbm.1, bf16[16,4096]{1,0:T(8,128)(2,1)} %b0_hbm.1, s32[1,1]{1,0:T(1,128)S(6)} %copy.13.cnt_ref, ...), custom_call_target="tpu_custom_call" | custom-call | tf_op jit(solution)/shard_map/pallas_call | solution.py:527
  146.0 1.4 copy.15
  147.4 1.3 copy.16

commit v10 on v2

--- a/solution.py
+++ b/solution.py
@@ -203,22 +203,29 @@
     mask[...] = (lane < live).astype(jnp.float32)
     tokens_live[...] = z_finish(0)
 
-    def rs_copy(it, way, h, odd, e, owner):
+    cut = width_in // 256 * 128 + 128
+    pieces_of = [(h, pl.ds(at, size)) for h in range(2) for at, size in ((0, cut), (cut, width_in - cut))]
+
+    def piece_of(ref, p):
+        h, cols = pieces_of[p]
+        return ref.at[h, :, cols]
+
+    def rs_copy(it, way, p, odd, e, owner):
         return pltpu.make_async_remote_copy(
-            src_ref=grad.at[it, owner, h],
-            dst_ref=slot.at[it, way, h, odd, e],
-            send_sem=rs_send.at[it, way, h, odd, e],
-            recv_sem=rs_recv.at[it, way, h, odd, e],
+            src_ref=piece_of(grad.at[it, owner], p),
+            dst_ref=piece_of(slot.at[it, way, odd, e], p),
+            send_sem=rs_send.at[it, way, p, odd, e],
+            recv_sem=rs_recv.at[it, way, p, odd, e],
             device_id={"dp": ring[odd][way]},
             device_id_type=MESH,
         )
 
-    def ag_copy(it, way, h, odd, t, owner):
+    def ag_copy(it, way, p, odd, t, owner):
         return pltpu.make_async_remote_copy(
-            src_ref=a_all.at[it, owner, h],
-            dst_ref=a_all.at[it, owner, h],
-            send_sem=ag_send.at[it, way, h, odd, t],
-            recv_sem=ag_recv.at[it, way, h, odd, t],
+            src_ref=piece_of(a_all.at[it, owner], p),
+            dst_ref=piece_of(a_all.at[it, owner], p),
+            send_sem=ag_send.at[it, way, p, odd, t],
+            recv_sem=ag_recv.at[it, way, p, odd, t],
             device_id={"dp": ring[odd][way]},
             device_id_type=MESH,
         )
@@ -233,8 +240,11 @@
             device_id_type=MESH,
         )
 
-    def long(way, h):
-        return way == h
+    def long(way, p):
+        return way == pieces_of[p][0]
+
+    def own_pieces(way):
+        return [p for p in range(4) if long(way, p)]
 
     far = at_z(half_n)
 
@@ -257,13 +267,14 @@
 
         def send_odd(e):
             owners = beside(half_n - 1 - 2 * e)
-            for h in range(2):
+            for p in range(4):
                 for way in range(2):
-                    rs_copy(it, way, h, 1, e, owners[way]).start()
+                    rs_copy(it, way, p, 1, e, owners[way]).start()
 
         local(far)
         for way in range(2):
-            rs_copy(it, way, way, 0, 0, far).start()
+            for p in own_pieces(way):
+                rs_copy(it, way, p, 0, 0, far).start()
         local_both(half_n - 1)
         send_odd(0)
         local_both(half_n - 2)
@@ -280,15 +291,15 @@
 
         for e in range(1, stops):
             owners = beside(half_n - 2 * e)
-            for h in range(2):
+            for p, (h, cols) in enumerate(pieces_of):
                 for way in range(2):
-                    rs_copy(it, way, h, 1, e - 1, owners[way]).wait_recv()
-                    total = grad[it, owners[way], h] + slot[it, way, h, 1, e - 1]
-                    if long(way, h) or e > 1:
-                        rs_copy(it, way, h, 0, e - 1, owners[way]).wait_recv()
-                        total = total + slot[it, way, h, 0, e - 1]
-                    grad[it, owners[way], h] = total
-                    rs_copy(it, way, h, 0, e, owners[way]).start()
+                    rs_copy(it, way, p, 1, e - 1, owners[way]).wait_recv()
+                    total = grad[it, owners[way], h, :, cols] + slot[it, way, 1, e - 1, h, :, cols]
+                    if long(way, p) or e > 1:
+                        rs_copy(it, way, p, 0, e - 1, owners[way]).wait_recv()
+                        total = total + slot[it, way, 0, e - 1, h, :, cols]
+                    grad[it, owners[way], h, :, cols] = total
+                    rs_copy(it, way, p, 0, e, owners[way]).start()
             if e < stops - 1:
                 local_both(half_n - 2 * e - 2)
                 local_both(half_n - 2 * e - 3)
@@ -302,72 +313,81 @@
                     pt_copy(it, way, 0, e, source).start()
                 pt_copy(it, way, 1, e, source).start()
                 pt_copy(it, way, 1, e - 1, source).wait_recv()
-        for h in range(2):
-            total = grad[it, z, h]
+        for p, (h, cols) in enumerate(pieces_of):
+            total = grad[it, z, h, :, cols]
             for odd in (1, 0):
                 for way in range(2):
-                    rs_copy(it, way, h, odd, stops - 1, z).wait_recv()
-                    total = total + slot[it, way, h, odd, stops - 1]
-            own[h] = own[h] - learn_rate * total
+                    rs_copy(it, way, p, odd, stops - 1, z).wait_recv()
+                    total = total + slot[it, way, odd, stops - 1, h, :, cols]
+            own[h, :, cols] = own[h, :, cols] - learn_rate * total
 
             @pl.when(it < ITERS - 1)
             def _():
-                a_all[it, z, h] = own[h]
+                a_all[it, z, h, :, cols] = own[h, :, cols]
                 for way in range(2):
-                    ag_copy(it, way, h, 0, 0, z).start()
+                    ag_copy(it, way, p, 0, 0, z).start()
+
+        def inner_total():
+            pt_copy(it, 0, 0, stops - 1, far).wait_recv()
+            for way in range(2):
+                pt_copy(it, way, 1, stops - 1, far).wait_recv()
+            tile = part[it, 0]
+            for j in range(1, n):
+                tile = tile + part[it, j]
+            return jnp.concatenate([tile[:, :nout], tile[:, nout:]], axis=0)
+
+        @pl.when(it == ITERS - 1)
+        def _():
+            inner_sum[...] += inner_total()
 
         @pl.when(it < ITERS - 1)
         def _():
-            for h in range(2):
-                for way in range(2):
-                    ag_copy(it, way, h, 1, 0, z).start()
-
-        pt_copy(it, 0, 0, stops - 1, far).wait_recv()
-        for way in range(2):
-            pt_copy(it, way, 1, stops - 1, far).wait_recv()
-        tile = part[it, 0]
-        for j in range(1, n):
-            tile = tile + part[it, j]
-        step_inner = jnp.concatenate([tile[:, :nout], tile[:, nout:]], axis=0)
-        inner_sum[...] += step_inner
-
-        @pl.when(it < ITERS - 1)
-        def _():
-            mixed[...] = mixed[...] - learn_rate * mm(step_inner, gram[...], NN, HIGH)
-            mixed_t[...] = mixed_t[...] - learn_rate * mm(gram[...], step_inner, NT, HIGH)
-            from_mixed()
-
             def project(owner):
                 rows = jnp.concatenate([a_all[it, owner, 0], a_all[it, owner, 1]], axis=0)
                 return mm(hv[owner], rows.astype(jnp.bfloat16), NT)
 
+            def send_between(t, sources):
+                for p in range(4):
+                    for way in range(2):
+                        ag_copy(it, way, p, 1, t, sources[way]).start()
+
+            def use_between(t):
+                owners = (at_z(2 * t + 1), at_z(n - 2 * t - 1))
+                for way in range(2):
+                    for p in range(4):
+                        ag_copy(it, way, p, 1, t, owners[way]).wait_recv()
+                    proj[...] += project(owners[way])
+
+            send_between(0, (z, z))
             proj[...] = project(z)
 
             for t in range(1, stops):
                 sources = (at_z(2 * t), at_z(n - 2 * t))
-                between = (at_z(2 * t - 1), at_z(n - 2 * t + 1))
-                for h in range(2):
+                for p in range(4):
                     for way in range(2):
-                        ag_copy(it, way, h, 0, t - 1, sources[way]).wait_recv()
-                        if long(way, h) or t < stops - 1:
-                            ag_copy(it, way, h, 0, t, sources[way]).start()
+                        ag_copy(it, way, p, 0, t - 1, sources[way]).wait_recv()
+                        if long(way, p) or t < stops - 1:
+                            ag_copy(it, way, p, 0, t, sources[way]).start()
+                if t == stops - 1:
+                    send_between(t, sources)
                 proj[...] += project(sources[0])
-                for h in range(2):
-                    for way in range(2):
-                        ag_copy(it, way, h, 1, t, sources[way]).start()
+                if t < stops - 1:
+                    send_between(t, sources)
                 proj[...] += project(sources[1])
-                for way in range(2):
-                    for h in range(2):
-                        ag_copy(it, way, h, 1, t - 1, between[way]).wait_recv()
-                    proj[...] += project(between[way])
-            between = (at_z(half_n - 1), at_z(n - half_n + 1))
+                use_between(t - 1)
+                if t == 1:
+                    step_inner = inner_total()
+                    inner_sum[...] += step_inner
+                if t == 2:
+                    mixed[...] = mixed[...] - learn_rate * mm(step_inner, gram[...], NN, HIGH)
+                    mixed_t[...] = mixed_t[...] - learn_rate * mm(gram[...], step_inner, NT, HIGH)
+                if t == stops - 1:
+                    from_mixed()
             for way in range(2):
-                for h in range(2):
-                    ag_copy(it, way, h, 1, stops - 1, between[way]).wait_recv()
-                proj[...] += project(between[way])
-            for way in range(2):
-                ag_copy(it, way, way, 0, stops - 1, far).wait_recv()
+                for p in own_pieces(way):
+                    ag_copy(it, way, p, 0, stops - 1, far).wait_recv()
             proj[...] += project(far)
+            use_between(stops - 1)
 
         return 0
 
@@ -446,10 +466,10 @@
     def drain_step(it, _):
         for way in range(2):
             for e in range(stops):
-                for h in range(2):
-                    if long(way, h) or e > 0:
-                        rs_copy(it, way, h, 0, e, z).wait_send()
-                    rs_copy(it, way, h, 1, e, z).wait_send()
+                for p in range(4):
+                    if long(way, p) or e > 0:
+                        rs_copy(it, way, p, 0, e, z).wait_send()
+                    rs_copy(it, way, p, 1, e, z).wait_send()
                 if way == 0 or e < stops - 1:
                     pt_copy(it, way, 0, e, z).wait_send()
                 pt_copy(it, way, 1, e, z).wait_send()
@@ -457,10 +477,10 @@
             @pl.when(it < ITERS - 1)
             def _():
                 for e in range(stops):
-                    for h in range(2):
-                        if long(way, h) or e < stops - 1:
-                            ag_copy(it, way, h, 0, e, z).wait_send()
-                        ag_copy(it, way, h, 1, e, z).wait_send()
+                    for p in range(4):
+                        if long(way, p) or e < stops - 1:
+                            ag_copy(it, way, p, 0, e, z).wait_send()
+                        ag_copy(it, way, p, 1, e, z).wait_send()
 
         return 0
 
@@ -535,7 +555,7 @@
             pltpu.VMEM((rank, rank), f32),
             pltpu.VMEM((rank, tokens), f32),
             pltpu.VMEM((ITERS, n, 2, half, width_in), f32),
-            pltpu.VMEM((ITERS, 2, 2, 2, stops, half, width_in), f32),
+            pltpu.VMEM((ITERS, 2, 2, stops, 2, half, width_in), f32),
             pltpu.VMEM((ITERS - 1, n, 2, half, width_in), f32),
             pltpu.VMEM((2, half, width_in), f32),
             pltpu.VMEM((ITERS, n, half, 128), f32),
@@ -545,10 +565,10 @@
             pltpu.VMEM((rank, 1, width), f32),
             dma((6,)),
             dma((n,)),
-            dma((ITERS, 2, 2, 2, stops)),
-            dma((ITERS, 2, 2, 2, stops)),
-            dma((ITERS - 1, 2, 2, 2, stops)),
-            dma((ITERS - 1, 2, 2, 2, stops)),
+            dma((ITERS, 2, 4, 2, stops)),
+            dma((ITERS, 2, 4, 2, stops)),
+            dma((ITERS - 1, 2, 4, 2, stops)),
+            dma((ITERS - 1, 2, 4, 2, stops)),
             dma((ITERS, 2, 2, stops)),
             dma((ITERS, 2, 2, stops)),
             dma((2, n)),

time: 143 us -> 142 us (level)
  no operation moved by 1% of the time
where the time goes in v10:
time: 142 us
  Pallas kernels  137 us (96%)
  local copies, waits for them, and re-layouts  2.77 us (2%)
  between operations  1.93 us (1%)
    pallas_call x1, Pallas kernels, on_device(): pl.pallas_call(functools.partial(kernel, n, clients, out_scale), out_shap...  137 us

profile of v10, /device:TPU:1, one launch (start us, length us, event | category | flops | bytes accessed | tf_op | source)
XLA Modules:
  0.0 141.7 jit_solution(4331729025162026331)
XLA Ops:
  1.9 137.0 %shard_map.104 = (f32[16,896]{1,0:T(8,128)}, f32[16,256]{1,0:T(8,128)}) custom-call(bf16[1,128,14336]{2,1,0:T(8,128)(2,1)} %hid_ref.1, bf16[64,128]{1,0:T(8,128)(2,1)} %bitcast.5, bf16[64,4096]{1,0:T(8,128)(2,1)} %bitcast.4, bf16[16,14336]{1,0:T(8,128)(2,1)} %a0_hbm.1, bf16[16,4096]{1,0:T(8,128)(2,1)} %b0_hbm.1, s32[1,1]{1,0:T(1,128)S(6)} %copy.13.cnt_ref, ...), custom_call_target="tpu_custom_call" | custom-call | tf_op jit(solution)/shard_map/pallas_call | solution.py:529
  138.9 1.4 %copy.15 = f32[16,896]{1,0:T(8,128)} copy(f32[16,896]{1,0:T(8,128)} %get-tuple-element.4) | data formatting | bytes 114688
  140.3 1.3 copy.16

commit v11 on v10

--- a/solution.py
+++ b/solution.py
@@ -206,14 +206,16 @@
     cut = width_in // 256 * 128 + 128
     pieces_of = [(h, pl.ds(at, size)) for h in range(2) for at, size in ((0, cut), (cut, width_in - cut))]
 
-    def piece_of(ref, p):
+    def piece_of(ref, odd, p):
+        if odd:
+            return ref.at[p]
         h, cols = pieces_of[p]
         return ref.at[h, :, cols]
 
     def rs_copy(it, way, p, odd, e, owner):
         return pltpu.make_async_remote_copy(
-            src_ref=piece_of(grad.at[it, owner], p),
-            dst_ref=piece_of(slot.at[it, way, odd, e], p),
+            src_ref=piece_of(grad.at[it, owner], odd, p),
+            dst_ref=piece_of(slot.at[it, way, odd, e], odd, p),
             send_sem=rs_send.at[it, way, p, odd, e],
             recv_sem=rs_recv.at[it, way, p, odd, e],
             device_id={"dp": ring[odd][way]},
@@ -222,8 +224,8 @@
 
     def ag_copy(it, way, p, odd, t, owner):
         return pltpu.make_async_remote_copy(
-            src_ref=piece_of(a_all.at[it, owner], p),
-            dst_ref=piece_of(a_all.at[it, owner], p),
+            src_ref=piece_of(a_all.at[it, owner], odd, p),
+            dst_ref=piece_of(a_all.at[it, owner], odd, p),
             send_sem=ag_send.at[it, way, p, odd, t],
             recv_sem=ag_recv.at[it, way, p, odd, t],
             device_id={"dp": ring[odd][way]},
@@ -267,9 +269,9 @@
 
         def send_odd(e):
             owners = beside(half_n - 1 - 2 * e)
-            for p in range(4):
+            for h in range(2):
                 for way in range(2):
-                    rs_copy(it, way, p, 1, e, owners[way]).start()
+                    rs_copy(it, way, h, 1, e, owners[way]).start()
 
         local(far)
         for way in range(2):
@@ -293,7 +295,8 @@
             owners = beside(half_n - 2 * e)
             for p, (h, cols) in enumerate(pieces_of):
                 for way in range(2):
-                    rs_copy(it, way, p, 1, e - 1, owners[way]).wait_recv()
+                    if p % 2 == 0:
+                        rs_copy(it, way, h, 1, e - 1, owners[way]).wait_recv()
                     total = grad[it, owners[way], h, :, cols] + slot[it, way, 1, e - 1, h, :, cols]
                     if long(way, p) or e > 1:
                         rs_copy(it, way, p, 0, e - 1, owners[way]).wait_recv()
@@ -317,7 +320,10 @@
             total = grad[it, z, h, :, cols]
             for odd in (1, 0):
                 for way in range(2):
-                    rs_copy(it, way, p, odd, stops - 1, z).wait_recv()
+                    if not odd:
+                        rs_copy(it, way, p, 0, stops - 1, z).wait_recv()
+                    elif p % 2 == 0:
+                        rs_copy(it, way, h, 1, stops - 1, z).wait_recv()
                     total = total + slot[it, way, odd, stops - 1, h, :, cols]
             own[h, :, cols] = own[h, :, cols] - learn_rate * total
 
@@ -347,15 +353,15 @@
                 return mm(hv[owner], rows.astype(jnp.bfloat16), NT)
 
             def send_between(t, sources):
-                for p in range(4):
+                for h in range(2):
                     for way in range(2):
-                        ag_copy(it, way, p, 1, t, sources[way]).start()
+                        ag_copy(it, way, h, 1, t, sources[way]).start()
 
             def use_between(t):
                 owners = (at_z(2 * t + 1), at_z(n - 2 * t - 1))
                 for way in range(2):
-                    for p in range(4):
-                        ag_copy(it, way, p, 1, t, owners[way]).wait_recv()
+                    for h in range(2):
+                        ag_copy(it, way, h, 1, t, owners[way]).wait_recv()
                     proj[...] += project(owners[way])
 
             send_between(0, (z, z))
@@ -469,7 +475,8 @@
                 for p in range(4):
                     if long(way, p) or e > 0:
                         rs_copy(it, way, p, 0, e, z).wait_send()
-                    rs_copy(it, way, p, 1, e, z).wait_send()
+                    if p < 2:
+                        rs_copy(it, way, p, 1, e, z).wait_send()
                 if way == 0 or e < stops - 1:
                     pt_copy(it, way, 0, e, z).wait_send()
                 pt_copy(it, way, 1, e, z).wait_send()
@@ -480,7 +487,8 @@
                     for p in range(4):
                         if long(way, p) or e < stops - 1:
                             ag_copy(it, way, p, 0, e, z).wait_send()
-                        ag_copy(it, way, p, 1, e, z).wait_send()
+                        if p < 2:
+                            ag_copy(it, way, p, 1, e, z).wait_send()
 
         return 0
 

time: 142 us -> 142 us (level)
  no operation moved by 1% of the time
where the time goes in v11:
time: 142 us
  Pallas kernels  137 us (96%)
  local copies, waits for them, and re-layouts  2.77 us (2%)
  between operations  1.93 us (1%)
    pallas_call x1, Pallas kernels, on_device(): pl.pallas_call(functools.partial(kernel, n, clients, out_scale), out_shap...  137 us

profile of v11, /device:TPU:1, one launch (start us, length us, event | category | flops | bytes accessed | tf_op | source)
XLA Modules:
  0.0 141.9 jit_solution(17807525043811149110)
XLA Ops:
  1.9 137.2 %shard_map.104 = (f32[16,896]{1,0:T(8,128)}, f32[16,256]{1,0:T(8,128)}) custom-call(bf16[1,128,14336]{2,1,0:T(8,128)(2,1)} %hid_ref.1, bf16[64,128]{1,0:T(8,128)(2,1)} %bitcast.5, bf16[64,4096]{1,0:T(8,128)(2,1)} %bitcast.4, bf16[16,14336]{1,0:T(8,128)(2,1)} %a0_hbm.1, bf16[16,4096]{1,0:T(8,128)(2,1)} %b0_hbm.1, s32[1,1]{1,0:T(1,128)S(6)} %copy.13.cnt_ref, ...), custom_call_target="tpu_custom_call" | custom-call | tf_op jit(solution)/shard_map/pallas_call | solution.py:537
  139.1 1.4 %copy.15 = f32[16,896]{1,0:T(8,128)} copy(f32[16,896]{1,0:T(8,128)} %get-tuple-element.4) | data formatting | bytes 114688
  140.6 1.3 copy.16
